TPU v7x, 32 devices: a whole 2x2x4 slice. The times are simulated.
32 devices in a mesh: lvl: 2 (over y), row: 16 (over z, x, core).
Axes of the slice: x: 2, y: 2, z: 4, core: 2. Of those that a mesh axis runs over, the one named last changes fastest.
Arguments:
- node_latent: float32 [8192, 512], P('row'), may hold values from -6 to 6
- edge_latent: float32 [81920, 512], P(('lvl', 'row')), may hold values from -6 to 6
- senders: int32 [81920], P(('lvl', 'row')), may hold values from 0 to 8191, as said below
- receivers: int32 [81920], P(('lvl', 'row')), may hold values from 0 to 8191, as said below
- live_edges: int32 [32], P(('lvl', 'row')), may hold values from 640 to 2560, as said below
- edge_w1: bfloat16 [2, 1536, 512], replicated, may hold values from -0.15625 to 0.15625
- edge_b1: float32 [2, 512], replicated, may hold values from -3 to 3
- edge_w2: bfloat16 [2, 512, 512], replicated, may hold values from -0.25 to 0.25
- edge_b2: float32 [2, 512], replicated, may hold values from -3 to 3
- edge_gain: float32 [2, 512], replicated, may hold values from 0.5 to 1.5
- edge_shift: float32 [2, 512], replicated, may hold values from -2 to 2
- node_w1: bfloat16 [2, 1024, 512], replicated, may hold values from -0.1875 to 0.1875
- node_b1: float32 [2, 512], replicated, may hold values from -3 to 3
- node_w2: bfloat16 [2, 512, 512], replicated, may hold values from -0.25 to 0.25
- node_b2: float32 [2, 512], replicated, may hold values from -3 to 3
- node_gain: float32 [2, 512], replicated, may hold values from 0.5 to 1.5
- node_shift: float32 [2, 512], replicated, may hold values from -2 to 2
- node_cotangent: float32 [8192, 512], P('row'), may hold values from -6 to 6
- edge_cotangent: float32 [81920, 512], P(('lvl', 'row')), may hold values from -6 to 6
Outputs:
- node_out: float32 [8192, 512], P('row')
- edge_out: float32 [81920, 512], P(('lvl', 'row'))
- node_grad: float32 [8192, 512], P('row')
- edge_grad: float32 [81920, 512], P(('lvl', 'row'))
- grad_edge_w1: float32 [2, 1536, 512], replicated
- grad_edge_b1: float32 [2, 512], replicated
- grad_edge_w2: float32 [2, 512, 512], replicated
- grad_edge_b2: float32 [2, 512], replicated
- grad_edge_gain: float32 [2, 512], replicated
- grad_edge_shift: float32 [2, 512], replicated
- grad_node_w1: float32 [2, 1024, 512], replicated
- grad_node_b1: float32 [2, 512], replicated
- grad_node_w2: float32 [2, 512, 512], replicated
- grad_node_b2: float32 [2, 512], replicated
- grad_node_gain: float32 [2, 512], replicated
- grad_node_shift: float32 [2, 512], replicated
- stream_rms: float32 [2, 4], replicated
Inputs may be any that keep to these rules, and one draw needn't show every extreme that they name: Edge block b (slots b * 2560 to (b + 1) * 2560 - 1) has receivers in node rows (b mod 16) * 512 to (b mod 16 + 1) * 512 - 1, never falling within the block, its first slot at the first of these rows and its last slot at the last; padded slots also carry such receivers. In each edge block, for each r, exactly 160 slots have senders in node rows r * 512 to (r + 1) * 512 - 1. `live_edges`: some edge block has all 2560 slots live in every draw.
All inputs are finite; a program needn't handle non-finite values.
Results may differ from a plain program's by a relative error of at most 0.02.
Values may be sent and summed in bfloat16 or wider, within the bound.
A program may use at most 320 MiB of HBM per device.

v0:
```python
import functools

import jax
import jax.numpy as jnp
from jax import lax
from jax.experimental import pallas as pl
from jax.experimental.pallas import tpu as pltpu
from jax.sharding import PartitionSpec as P

MESH = pl.DeviceIdType.MESH
NORM_EPS = 1e-05
F32 = jnp.float32
BF16 = jnp.bfloat16
VMEM_BYTES = 61 * 2**20


WORK_ORDER = (
    (
        1089728, 289296, 536069, 551556, 141360, 612561, 159764, 1528408, 356492, 400397,
        858841, 422440, 750249, 990892, 1707549, 1799737, 2097129,
    ),
    (
        1089728, 1392676, 131237, 197853, 1464864, 215760, 1448028, 272952, 399521, 881172,
        290876, 745128, 724581, 482457, 1774801, 1717985, 2097129,
    ),
)
ORDER = (
    (
        266400, 82449, 788882, 135431, 104611, 150052, 820491, 853654, 609459, 445454,
        201638, 755629, 347034, 923038, 693433, 481974, 464424, 513978, 908990, 974399,
    ),
    (
        4616, 168577, 183049, 854950, 200706, 541080, 645773, 661524, 559118, 804778,
        281910, 940344, 414866, 774588, 1006515, 495253, 1018298, 1036204, 744878, 445995,
    ),
)
PLAIN_ORDER = (
    (
        524816, 133680, 394788, 465448, 990252,
    ),
    (
        328704, 526372, 658444, 464948, 990252,
    ),
)


NEAREST = ((0, 1, 2, 3), (1, 0, 2, 3), (2, 3, 1, 0), (3, 2, 1, 0))


class Grid:
    def __init__(self, levels, rows):
        self.L, self.R = levels, rows
        self.Z = 4
        self.X = rows // (2 * self.Z)
        self.l = lax.axis_index("lvl")
        row = lax.axis_index("row")
        self.row = row
        self.core = lax.rem(row, 2)
        self.x = lax.rem(row // 2, self.X)
        self.z = row // (2 * self.X)
        self.up = self.z < self.Z - 1
        self.down = self.z > 0

    def block(self, z, x, core):
        return (z * self.X + x) * 2 + core

    def mate(self):
        return (self.l, self.block(self.z, self.x, 1 - self.core))

    def at_z(self, z):
        return (self.l, self.block(jnp.clip(z, 0, self.Z - 1), self.x, self.core))

    def x_other(self, i):
        x = lax.rem(self.x + i, self.X)
        return x, (self.l, self.block(self.z, x, self.core))

    def l_other(self, i):
        l = lax.rem(self.l + i, self.L)
        return l, (l, self.row)

    def nth(self, k, z=None):
        z_here = self.z if z is None else z
        order = NEAREST
        out = jnp.int32(0)
        for z in range(4):
            for j in range(4):
                if order[z][j]:
                    out = jnp.where((z_here == z) & (k == j), order[z][j], out)
        return out

    def local(self, zk, z=None):
        return (zk // 2) == lax.rem(self.z if z is None else z, 2)

    def corner_z(self, q):
        side = lax.rem(lax.rem(self.z, 2) + q // 2, 2)
        return side * 2 + lax.rem(q, 2)

    def pair_z(self):
        return self.z + 1 - 2 * lax.rem(self.z, 2)

    def greet(self):
        barrier = pltpu.get_barrier_semaphore()

        def hello(who):
            pl.semaphore_signal(barrier, inc=1, device_id=who, device_id_type=MESH)

        hello(self.mate())
        for i in range(1, self.X):
            hello(self.x_other(i)[1])
        for i in range(1, self.L):
            hello(self.l_other(i)[1])
        pl.when(self.up)(lambda: hello(self.at_z(self.z + 1)))
        pl.when(self.down)(lambda: hello(self.at_z(self.z - 1)))
        pl.semaphore_wait(barrier, self.X + self.L - 1 + self.up.astype(jnp.int32) + self.down.astype(jnp.int32))


def only(when, act):
    if when is None:
        act()
    else:
        pl.when(when)(act)


def cuts(h):
    first = -(-h // 32) * 16
    return ((0, first), (first, h - first)) if h > first else ((0, h),)


class Gather:
    def __init__(self, grid, table, h, send_sem, recv_sem):
        self.g, self.table, self.h = grid, table, h
        self.cuts = cuts(h)
        self.send_sem, self.recv_sem = send_sem, recv_sem
        X, L = grid.X, grid.L
        self.per_column = X + L + 1
        self.per_sides = 2 * (X - 1) * (L - 1) + X - 1 + L - 1
        self.at_sides = 4 * self.per_column
        self.at_corners = self.at_sides + 4 * self.per_sides
        self.drain = False

    @staticmethod
    def sends(levels, rows):
        X, L = rows // 8, levels
        return 2 * (4 * (X + L + 1) + 4 * (2 * (X - 1) * (L - 1) + X + L - 2) + 8 * (X - 1) * (L - 1))

    def slot(self, block, l, s=None):
        start, size = (0, self.h) if s is None else self.cuts[s]
        return self.table.at[pl.ds(pl.multiple_of((block * self.g.L + l) * self.h + start, 16), size)]

    def push(self, at, block, l, s, who, when=None):
        place = self.slot(block, l, s)
        copy = pltpu.make_async_remote_copy(
            place, place, self.send_sem.at[2 * at + s], self.recv_sem.at[(block * self.g.L + l) * 2 + s], device_id=who, device_id_type=MESH
        )
        only(when, copy.wait_send if self.drain else copy.start)

    def arrived(self, block, l, s):
        if self.drain:
            return
        place = self.slot(block, l, s)
        pltpu.make_async_remote_copy(
            place, place, self.send_sem.at[0], self.recv_sem.at[(block * self.g.L + l) * 2 + s], device_id=self.g.mate(), device_id_type=MESH
        ).wait_recv()

    def column(self, k, s, own=False):
        g = self.g
        zk = g.nth(k)
        block = g.block(zk, g.x, g.core)
        at = k * self.per_column
        if not own:
            self.arrived(block, g.l, s)
        self.push(at, block, g.l, s, g.at_z(g.z + 1), g.up & (zk <= g.z))
        self.push(at + 1, block, g.l, s, g.at_z(g.z - 1), g.down & (zk >= g.z))
        for i in range(1, g.X):
            self.push(at + 1 + i, block, g.l, s, g.x_other(i)[1])
        for j in range(1, g.L):
            self.push(at + g.X + j, block, g.l, s, g.l_other(j)[1])
        self.push(at + g.X + g.L, block, g.l, s, g.mate())

    def sides(self, k, s):
        g = self.g
        zk = g.nth(k)
        even = lax.rem(zk, 2) == 0
        at = self.at_sides + k * self.per_sides
        for i in range(1, g.X):
            block = g.block(zk, g.x_other(i)[0], g.core)
            self.arrived(block, g.l, s)
            for j in range(1, g.L):
                self.push(at, block, g.l, s, g.l_other(j)[1], g.local(zk) & even)
                at = at + 1
            self.push(at, block, g.l, s, g.mate())
            at = at + 1
        for j in range(1, g.L):
            block = g.block(zk, g.x, g.core)
            l = g.l_other(j)[0]
            self.arrived(block, l, s)
            for i in range(1, g.X):
                self.push(at, block, l, s, g.x_other(i)[1], g.local(zk) & jnp.logical_not(even))
                at = at + 1
            self.push(at, block, l, s, g.mate())
            at = at + 1

    def corners(self, z, s, local):
        g = self.g
        q = lax.rem(z, 2) + (0 if local else 2)
        for i in range(1, g.X):
            block = g.block(z, lax.rem(g.x + i, g.X), g.core)
            for j in range(1, g.L):
                l = g.l_other(j)[0]
                at = self.at_corners + ((q * (g.X - 1) + i - 1) * (g.L - 1) + j - 1) * 2
                self.arrived(block, l, s)
                if local:
                    self.push(at, block, l, s, g.at_z(g.pair_z()))
                self.push(at + 1, block, l, s, g.mate())

    def mates(self, z, x):
        for l in range(self.g.L):
            for s in range(len(self.cuts)):
                self.arrived(self.g.block(z, x, 1 - self.g.core), l, s)

    def begin(self):
        for s in range(len(self.cuts)):
            self.column(0, s, own=True)

    def wave(self, k, s):
        g = self.g
        pl.when(k < 3)(lambda: self.column(k + 1, s))
        pl.when(k < 4)(lambda: self.sides(k, s))
        if g.L == 1:
            return
        two = len(self.cuts) == 2
        late = 1 - s if two else s
        back = 2 - s if two else 1
        for local, lag in ((True, back), (False, back + 1)):
            who = None if local else g.pair_z()
            kk = k - lag
            z = g.nth(jnp.clip(kk, 0, 3), who)
            pl.when((kk >= 0) & (kk < 4) & g.local(z, who))(lambda z=z, local=local: self.corners(z, late, local))

    def due(self, k, c):
        g = self.g
        own = c == 0
        far = c > g.X - 1
        off = jnp.where(own, 0, lax.rem(c - 1, max(g.X - 1, 1)) + 1)
        kk = jnp.where(own, k - 1, jnp.where(far, k - 3, k - 2))
        who = jnp.where(far, g.pair_z(), g.z)
        z = g.nth(jnp.clip(kk, 0, 3), who)
        there = (kk >= 0) & (kk < 4) & (own | g.local(z, who))
        return z, lax.rem(g.x + off, g.X), there

    def run(self, work=None, meanwhile=None):
        g = self.g
        parts = 2 * g.X - 1
        self.begin()

        def one(i, done):
            k, c = i // parts, lax.rem(i, parts)
            for s in range(len(self.cuts)):
                pl.when(c == s)(lambda s=s: self.wave(k, s))
            if meanwhile is not None:
                for at in range(3):
                    pl.when(i == at)(lambda at=at: meanwhile(at))
            z, x, there = self.due(k, c)

            def ready():
                self.mates(z, x)
                if work is not None:
                    work(z, x, done)

            pl.when(there)(ready)
            return done + there.astype(jnp.int32)

        lax.fori_loop(0, 7 * parts, one, jnp.int32(0))

    def finish(self):
        self.drain = True
        self.begin()

        def one(k, carry):
            for s in range(len(self.cuts)):
                self.wave(k, s)
            return carry

        lax.fori_loop(0, 7, one, 0)


class Courier:
    def __init__(self, grid, table, h, cuts, send_sem, recv_sem):
        self.g, self.table, self.h = grid, table, h
        self.cuts = cuts
        self.size = h // self.cuts
        self.send_sem, self.recv_sem = send_sem, recv_sem
        self.drain = False

    @staticmethod
    def kinds(levels, rows):
        X, L = rows // 8, levels
        return (X + L + 1, (X - 1) * L, (L - 1) * X, 3 * (X - 1) * (L - 1))

    @staticmethod
    def sends(levels, rows, cuts):
        return 4 * sum(Courier.kinds(levels, rows)) * cuts

    @staticmethod
    def receives(levels, rows, cuts):
        return levels * rows * cuts

    def at(self, kind, zk, n, s):
        counts = self.kinds(self.g.L, self.g.R)
        return (4 * sum(counts[:kind]) + zk * counts[kind] + n) * self.cuts + s

    def slot(self, block, l, s=0, size=None):
        start = (block * self.g.L + l) * self.h + s * self.size
        return self.table.at[pl.ds(pl.multiple_of(start, 16), size or self.size)]

    def own(self):
        return self.slot(self.g.row, self.g.l, 0, self.h)

    def push(self, at, block, l, s, who, when=None):
        place = self.slot(block, l, s)
        copy = pltpu.make_async_remote_copy(
            place,
            place,
            self.send_sem.at[at],
            self.recv_sem.at[(block * self.g.L + l) * self.cuts + s],
            device_id=who,
            device_id_type=MESH,
        )
        only(when, copy.wait_send if self.drain else copy.start)

    def arrived(self, block, l, s):
        if self.drain:
            return
        place = self.slot(block, l, s)
        pltpu.make_async_remote_copy(
            place,
            place,
            self.send_sem.at[0],
            self.recv_sem.at[(block * self.g.L + l) * self.cuts + s],
            device_id=self.g.mate(),
            device_id_type=MESH,
        ).wait_recv()

    def near(self, zk):
        z = self.g.z
        return (zk == z) | ((z == 0) & (zk == 1)) | ((z == 3) & (zk == 2))

    def even(self, zk):
        return lax.rem(jnp.where(self.g.z < 2, zk, 3 - zk), 2) == 0

    def column(self, zk, s, own=False):
        g = self.g
        block = g.block(zk, g.x, g.core)
        if not own:
            self.arrived(block, g.l, s)
        self.push(self.at(0, zk, 0, s), block, g.l, s, g.at_z(g.z + 1), g.up & (zk <= g.z))
        self.push(self.at(0, zk, 1, s), block, g.l, s, g.at_z(g.z - 1), g.down & (zk >= g.z))
        for i in range(1, g.X):
            self.push(self.at(0, zk, 1 + i, s), block, g.l, s, g.x_other(i)[1])
        for j in range(1, g.L):
            self.push(self.at(0, zk, g.X + j, s), block, g.l, s, g.l_other(j)[1])
        self.push(self.at(0, zk, g.X + g.L, s), block, g.l, s, g.mate())

    def side_x(self, zk, s):
        g = self.g
        n = 0
        for i in range(1, g.X):
            block = g.block(zk, g.x_other(i)[0], g.core)
            self.arrived(block, g.l, s)
            for j in range(1, g.L):
                self.push(self.at(1, zk, n, s), block, g.l, s, g.l_other(j)[1], self.near(zk) & self.even(zk))
                n += 1
            self.push(self.at(1, zk, n, s), block, g.l, s, g.mate())
            n += 1

    def side_l(self, zk, s):
        g = self.g
        block = g.block(zk, g.x, g.core)
        n = 0
        for j in range(1, g.L):
            l = g.l_other(j)[0]
            self.arrived(block, l, s)
            for i in range(1, g.X):
                self.push(self.at(2, zk, n, s), block, l, s, g.x_other(i)[1], self.near(zk) & jnp.logical_not(self.even(zk)))
                n += 1
            self.push(self.at(2, zk, n, s), block, l, s, g.mate())
            n += 1

    def corner(self, zk, s):
        g = self.g
        n = 0
        for i in range(1, g.X):
            block = g.block(zk, g.x_other(i)[0], g.core)
            for j in range(1, g.L):
                l = g.l_other(j)[0]
                self.arrived(block, l, s)
                self.push(self.at(3, zk, n, s), block, l, s, g.at_z(g.z + 1), (zk <= 1) & (g.z >= zk) & g.up)
                self.push(self.at(3, zk, n + 1, s), block, l, s, g.at_z(g.z - 1), (zk >= 2) & (g.z <= zk) & g.down)
                self.push(self.at(3, zk, n + 2, s), block, l, s, g.mate())
                n += 3

    def mates(self, zk, x):
        def one(i, carry):
            self.arrived(self.g.block(zk, x, 1 - self.g.core), i // self.cuts, lax.rem(i, self.cuts))
            return carry

        lax.fori_loop(0, self.g.L * self.cuts, one, 0)

    def run(self, tables, meanwhile=None, prepare=None, work=None):
        g = self.g
        for s in range(self.cuts):
            self.column(g.z, s, own=True)
        low = g.z < 2
        first = (g.z == 0) | (g.z == 3)

        def one(m, done):
            word = jnp.int32(0)
            for at, (a, b) in enumerate(zip(*tables)):
                word = jnp.where(m // 3 == at, jnp.where(first, a, b), word)
            byte = lax.rem(m, 3)
            code = lax.rem(jnp.where(byte == 0, word, jnp.where(byte == 1, word // 128, word // 16384)), 128)
            zk = lax.rem(code // 4, 4)
            zk = jnp.where(low, zk, 3 - zk)
            s = lax.rem(code, 4)
            kind = code // 16
            pl.when(kind == 0)(lambda: self.column(zk, s))
            if g.X > 1:
                pl.when(kind == 1)(lambda: self.side_x(zk, s))
            if g.L > 1:
                pl.when(kind == 2)(lambda: self.side_l(zk, s))
            if g.X > 1 and g.L > 1:
                pl.when(kind == 3)(lambda: self.corner(zk, s))
            if meanwhile is not None:
                for at in range(3):
                    pl.when(code == 64 + at)(lambda at=at: meanwhile(at))
            count = jnp.int32(0)
            if work is not None:
                for off in range(g.X):
                    x = lax.rem(g.x + off, g.X)
                    hit = s == (0 if off == 0 else 1)
                    pl.when((kind == 5) & hit)(lambda x=x: prepare(zk, x))

                    def full(x=x, off=off):
                        self.mates(zk, x)
                        work(zk, x, done + max(off - 1, 0))

                    pl.when((kind == 6) & hit)(full)
                count = jnp.where(kind == 6, jnp.where(s == 0, 1, g.X - 1), 0)
            return done + count

        lax.fori_loop(0, 3 * len(tables[0]), one, jnp.int32(0))
        if work is None:

            def last(i, carry):
                self.mates(i // g.X, lax.rem(i, g.X))
                return carry

            lax.fori_loop(0, 4 * g.X, last, 0)

    def finish(self):
        self.drain = True

        def one(i, carry):
            zk, s = i // self.cuts, lax.rem(i, self.cuts)
            self.column(zk, s)
            self.side_x(zk, s)
            self.side_l(zk, s)
            self.corner(zk, s)
            return carry

        lax.fori_loop(0, 4 * self.cuts, one, 0)


class Scatter:
    def __init__(self, grid, stage, inbox, h, send_sem, recv_sem):
        self.g, self.stage, self.inbox, self.h = grid, stage, inbox, h
        self.cuts = cuts(h)
        self.send_sem, self.recv_sem = send_sem, recv_sem
        X, L = grid.X, grid.L
        at = 0
        self.base = {}
        for name, count in self.parts(X, L):
            self.base[name] = at
            at += count
        at = 0
        self.out = {}
        for name, count in self.out_parts(X, L):
            self.out[name] = at
            at += count
        self.drain = False
        self.prepare()

    @staticmethod
    def parts(X, L):
        side = (X - 1) * (L - 1)
        return (("mate", 4 * X * L), ("pair", 2 * side), ("l2", side), ("x2", side), ("xc", 4 * (X - 1)), ("lc", 4 * (L - 1)), ("z", 5))

    @staticmethod
    def out_parts(X, L):
        side = (X - 1) * (L - 1)
        return (("mate", 4 * X * L), ("corner", 8 * side), ("xc", 4 * (X - 1)), ("lc", 4 * (L - 1)), ("z", 4))

    @staticmethod
    def receives(levels, rows):
        return sum(count for _, count in Scatter.parts(rows // 8, levels))

    @staticmethod
    def sends(levels, rows):
        return 2 * sum(count for _, count in Scatter.out_parts(rows // 8, levels))

    def slot(self, block, l, s=None):
        start, size = (0, self.h) if s is None else self.cuts[s]
        return self.stage.at[pl.ds(pl.multiple_of((block * self.g.L + l) * self.h + start, 16), size)]

    def push(self, out, block, l, s, at, who, when=None):
        start, size = self.cuts[s]
        copy = pltpu.make_async_remote_copy(
            self.slot(block, l, s),
            self.inbox.at[at, pl.ds(start, size)],
            self.send_sem.at[2 * out + s],
            self.recv_sem.at[2 * at + s],
            device_id=who,
            device_id_type=MESH,
        )
        only(when, copy.wait_send if self.drain else copy.start)

    def arrived(self, at, s):
        start, size = self.cuts[s]
        place = self.inbox.at[at, pl.ds(start, size)]
        pltpu.make_async_remote_copy(
            place, place, self.send_sem.at[0], self.recv_sem.at[2 * at + s], device_id=self.g.mate(), device_id_type=MESH
        ).wait_recv()

    def total(self, block, l, s, ats):
        start, size = self.cuts[s]
        for at in ats:
            self.arrived(at, s)
        out = self.slot(block, l, s)[...].astype(F32)
        for at in ats:
            out = out + self.inbox[at, start : start + size].astype(F32)
        return out

    def add(self, block, l, s, ats, when=None):
        if self.drain:
            return

        def act():
            self.slot(block, l, s)[...] = self.total(block, l, s, ats).astype(BF16)

        only(when, act)

    def each(self):
        return range(len(self.cuts))

    def to_mate(self, z, x):
        g = self.g
        for l in range(g.L):
            at = (z * g.X + x) * g.L + l
            for s in self.each():
                self.push(self.out["mate"] + at, g.block(z, x, 1 - g.core), l, s, self.base["mate"] + at, g.mate())

    def from_mate(self, z, x):
        g = self.g
        for l in range(g.L):
            for s in self.each():
                self.add(g.block(z, x, g.core), l, s, [self.base["mate"] + (z * g.X + x) * g.L + l])

    def corner_far(self, z, i):
        g = self.g
        block = g.block(z, lax.rem(g.x + i, g.X), g.core)
        for j in range(1, g.L):
            l = g.l_other(j)[0]
            spot = (lax.rem(z, 2) * (g.X - 1) + i - 1) * (g.L - 1) + j - 1
            for s in self.each():
                self.push(self.out["corner"] + spot, block, l, s, self.base["pair"] + spot, g.at_z(g.pair_z()))

    def corner_near(self, z, i):
        g = self.g
        x, x_dev = g.x_other(i)
        block = g.block(z, x, g.core)
        even = lax.rem(z, 2) == 0
        side = (g.X - 1) * (g.L - 1)
        for j in range(1, g.L):
            l, l_dev = g.l_other(j)
            spot = (lax.rem(z, 2) * (g.X - 1) + i - 1) * (g.L - 1) + j - 1
            out = self.out["corner"] + 2 * side + spot
            for s in self.each():
                self.add(block, l, s, [self.base["pair"] + spot])
                self.push(out, block, l, s, self.base["l2"] + (i - 1) * (g.L - 1) + g.L - j - 1, l_dev, even)
                self.push(out, block, l, s, self.base["x2"] + (g.X - i - 1) * (g.L - 1) + j - 1, x_dev, jnp.logical_not(even))

    def side_x(self, zk, i, waits):
        g = self.g
        x, x_dev = g.x_other(i)
        block = g.block(zk, x, g.core)
        ats = [self.base["l2"] + (i - 1) * (g.L - 1) + j - 1 for j in range(1, g.L)]
        for s in self.each():
            if ats and waits:
                self.add(block, g.l, s, ats)
            self.push(self.out["xc"] + zk * (g.X - 1) + i - 1, block, g.l, s, self.base["xc"] + zk * (g.X - 1) + g.X - i - 1, x_dev)

    def side_l(self, zk, waits):
        g = self.g
        block = g.block(zk, g.x, g.core)
        for j in range(1, g.L):
            l, l_dev = g.l_other(j)
            ats = [self.base["x2"] + (i - 1) * (g.L - 1) + j - 1 for i in range(1, g.X)]
            for s in self.each():
                if waits:
                    self.add(block, l, s, ats)
                self.push(self.out["lc"] + zk * (g.L - 1) + j - 1, block, l, s, self.base["lc"] + zk * (g.L - 1) + g.L - j - 1, l_dev)

    def around(self, zk):
        g = self.g
        ats = [self.base["xc"] + zk * (g.X - 1) + i - 1 for i in range(1, g.X)]
        return ats + [self.base["lc"] + zk * (g.L - 1) + j - 1 for j in range(1, g.L)]

    def column(self, zk):
        g = self.g
        block = g.block(zk, g.x, g.core)
        behind = jnp.where(zk > g.z, g.down, g.up)
        near = jnp.abs(zk - g.z) == 1
        spot = jnp.where(near & (zk < g.z), 4, zk)
        for s in self.each():
            self.add(block, g.l, s, self.around(zk))
            self.add(block, g.l, s, [self.base["z"] + zk], behind)
            self.push(self.out["z"] + zk, block, g.l, s, self.base["z"] + spot, g.at_z(jnp.where(zk > g.z, g.z + 1, g.z - 1)))

    def last(self, out):
        g = self.g
        for s in self.each():
            start, size = self.cuts[s]
            out[start : start + size, :] = self.total(g.row, g.l, s, self.around(g.z))
            for at, there in ((self.base["z"] + g.z, g.down), (self.base["z"] + 4, g.up)):

                def take(at=at, s=s, start=start, size=size):
                    self.arrived(at, s)
                    out[start : start + size, :] += self.inbox[at, start : start + size].astype(F32)

                pl.when(there)(take)

    @staticmethod
    def plan(X, hop=2):
        orders, spots = [], []
        for z in range(4):
            corners = (3, 2, 1, 0) if z < 2 else (0, 1, 2, 3)
            own = tuple(reversed(NEAREST[z]))
            order = []
            for j in range(4):
                order += [(corners[j], off) for off in range(1, X)] + [(own[j], 0)]
            orders.append(order)
            spots.append(({zk: max(m for m, (a, off) in enumerate(order) if a == zk and off) for zk in range(4)},
                          {zk: order.index((zk, 0)) for zk in range(4)}))
        names = ("far", "sx", "sl", "near", "sx_late", "sl_late", "column")
        due = [{name: {} for name in names} for _ in range(4)]

        def put(z, name, zk, step):
            while step in due[z][name]:
                step += 1
            due[z][name][step] = zk
            return step

        sides = [{}, {}, {}, {}]
        for z in range(4):
            pair = z + 1 - 2 * (z % 2)
            for zk in sorted(range(4), key=lambda a: spots[z][0][a]):
                near = zk // 2 == z % 2
                corner, own = spots[z][0][zk] + 1, spots[z][1][zk] + 1
                ready = put(z, "near", zk, max(corner, spots[pair][0][zk] + 1 + hop)) if near else put(z, "far", zk, corner)
                sx = put(z, "sx_late", zk, ready + hop) if near and zk % 2 == 0 else put(z, "sx", zk, corner)
                sl = put(z, "sl_late", zk, max(ready + hop, own)) if near and zk % 2 else put(z, "sl", zk, own)
                sides[z][zk] = max(sx, sl)
        for zk in range(4):
            for chain in (range(0, zk), range(3, zk, -1)):
                before = 0
                for z in chain:
                    before = put(z, "column", zk, max(sides[z][zk], before) + hop)
        steps = 1 + max(step for z in range(4) for name in names for step in due[z][name])
        return orders, due, steps

    def prepare(self):
        self.orders, self.due, self.steps = self.plan(self.g.X)
        self.blocks = 4 * self.g.X

    def pick(self, tables, m):
        out = jnp.int32(-1)
        for z in range(4):
            for at, value in tables[z].items():
                out = jnp.where((self.g.z == z) & (m == at), value, out)
        return out

    def place(self, m):
        g = self.g
        code = self.pick([{at: zk * g.X + off for at, (zk, off) in enumerate(order)} for order in self.orders], m)
        return code // g.X, lax.rem(g.x + lax.rem(code, g.X), g.X)

    def step(self, m):
        g = self.g

        def first():
            self.to_mate(*self.place(m))

        def second():
            self.from_mate(*self.place(m - 1))

        pl.when(m < self.blocks)(first)
        pl.when((m >= 1) & (m <= self.blocks))(second)

        def send(name, act, over_x):
            zk = self.pick([due[name] for due in self.due], m)

            def go():
                if over_x:
                    for i in range(1, g.X):
                        act(zk, i)
                else:
                    act(zk)

            pl.when(zk >= 0)(go)

        send("column", self.column, False)
        send("sl_late", lambda zk: self.side_l(zk, True), False)
        send("sx_late", lambda zk, i: self.side_x(zk, i, True), True)
        if g.L > 1:
            send("near", self.corner_near, True)
            send("far", self.corner_far, True)
        send("sl", lambda zk: self.side_l(zk, False), False)
        send("sx", lambda zk, i: self.side_x(zk, i, False), True)

    def go(self, m, ahead):
        self.step(m)

        def wait():
            self.drain = True
            self.step(m - ahead)
            self.drain = False

        pl.when(m >= ahead)(wait)

    def run(self, work=None, ahead=4, steps=None):
        def one(m, carry):
            if work is not None:
                work(m)
            self.go(m, ahead)
            return carry

        self.steps = steps or self.steps
        self.ahead = ahead
        lax.fori_loop(0, self.steps, one, 0)

    def finish(self):
        self.drain = True

        def one(m, carry):
            self.step(m)
            return carry

        lax.fori_loop(self.steps - self.ahead, self.steps, one, 0)


def dot(left, right):
    return jnp.dot(left, right, preferred_element_type=F32)


def dot_nt(left, right):
    return lax.dot_general(left, right, (((1,), (1,)), ((), ())), preferred_element_type=F32)


def dot_tn(left, right):
    return lax.dot_general(left, right, (((0,), (0,)), ((), ())), preferred_element_type=F32)


def fold(values):
    rows, width = values.shape
    return jnp.sum(values.reshape(rows // 8, 8, width), axis=0)


def norm_parts(values):
    average = jnp.mean(values, axis=-1, keepdims=True)
    centered = values - average
    scale = lax.rsqrt(jnp.mean(centered * centered, axis=-1, keepdims=True) + NORM_EPS)
    return centered * scale, scale


def norm_back(normed, scale, d_normed):
    mean_d = jnp.mean(d_normed, axis=-1, keepdims=True)
    mean_dn = jnp.mean(d_normed * normed, axis=-1, keepdims=True)
    return scale * (d_normed - mean_d - normed * mean_dn)


def silu_back(pre, d_active):
    gate = lax.logistic(pre)
    return d_active * (gate * (1.0 + pre * (1.0 - gate)))


def find_places(row_total, node_count, some, senders, receivers, live, place, side, facts_out, counts):
    tiles = senders.shape[0]
    group = tiles * 128 // row_total
    first = lax.axis_index("row") * node_count
    lane = lax.broadcasted_iota(jnp.int32, (128, 128), 1)
    sub = lax.broadcasted_iota(jnp.int32, (128, 128), 0)
    before = (sub < lane).astype(BF16)
    owner_ids = lax.broadcasted_iota(jnp.int32, (row_total, 128), 0)
    carry = owner_ids[:, :1].astype(F32) * group if some[0] == 0 else counts[:, 0:1]
    for tile in some:
        send = senders[tile : tile + 1, :]
        recv = receivers[tile : tile + 1, :] - first
        owner = lax.div(send, node_count)
        local = send - owner * node_count
        mine = owner_ids == owner
        ranks = dot(mine.astype(BF16), before) + carry
        spot = jnp.sum(jnp.where(mine, ranks, 0.0), axis=0, keepdims=True)
        carry = carry + jnp.sum(mine.astype(F32), axis=1, keepdims=True)
        place[tile : tile + 1, :] = spot.astype(jnp.int32)
        alive = (lane[:1] + tile * 128 < live[0, 0]).astype(jnp.int32)
        facts = jnp.where(sub == 0, lax.div(local, 16), 0)
        facts = jnp.where(sub == 1, lax.rem(local, 16), facts)
        facts = jnp.where(sub == 2, lax.div(recv, 16), facts)
        facts = jnp.where(sub == 3, lax.rem(recv, 16), facts)
        facts = jnp.where(sub == 4, alive, facts).astype(F32)
        side[:, pl.ds(tile * 128, 128)] = facts[:16].astype(BF16)
        facts_out[pl.ds(tile * 128, 128), :] = facts.T.astype(BF16)
    counts[...] = jnp.broadcast_to(carry, counts.shape)


def picker(place, start, size):
    ids = lax.broadcasted_iota(jnp.int32, (size, 128), 0) + start
    return jnp.concatenate([(ids == place[tile : tile + 1, :]).astype(BF16) for tile in range(place.shape[0])], axis=1)


def one_hot_cols(ids, count):
    lanes = lax.broadcasted_iota(jnp.int32, (ids.shape[0], count), 1).astype(F32)
    return (ids == lanes).astype(BF16)


def one_hot_rows(ids, count):
    subs = lax.broadcasted_iota(jnp.int32, (count, ids.shape[1]), 0).astype(F32)
    return (ids == subs).astype(BF16)


def load_all(pairs, sems):
    copies = [pltpu.make_async_copy(src, dst, sems.at[i]) for i, (src, dst) in enumerate(pairs)]
    for copy in copies:
        copy.start()
    return copies


def forward_kernel(
    layer, levels, rows, first_layer, *refs
):
    (node, b1, b2, gain, shift, nb1, nb2, ngain, nshift, w1_all, w2_all, nw1_all, nw2_all, plain_all) = refs[:14]
    refs = refs[14:]
    if first_layer:
        senders, receivers, live = refs[:3]
        refs = refs[3:]
    else:
        place, rows_of, cols_all, edges_all, before_all = refs[:5]
        refs = refs[5:]
    sent_out, pre_out, normed_out, update_out, moved_out = refs[:5]
    refs = refs[5:]
    if first_layer:
        edges_out, place, rows_of, cols = refs[:4]
        refs = refs[4:]
    scale_out, block_out, node_out, recv_out, npre_out, nnormed_out, nscale_out, tally = refs[:8]
    (
        table, total, cast, near, far, w1, w2, nw1, nw2, plain, joined, ordered, out_buf, scale_buf,
        load_sem, out_sem, moved_sem, send_sem, recv_sem, near_send, near_recv,
    ) = refs[8:29]
    if first_layer:
        side, counts = refs[29:]
    else:
        cols, edges, before = refs[29:]
    g = Grid(levels, rows)
    h, width = node_out.shape
    if first_layer:
        node = node.at[pl.ds(pl.multiple_of(g.l * h, h), h)]
    count = plain.shape[0]
    group = count // rows
    node_count = h * levels
    pairs = ((plain_all, plain), (w1_all.at[layer], w1), (w2_all.at[layer], w2), (nw1_all.at[layer], nw1), (nw2_all.at[layer], nw2))
    if not first_layer:
        pairs += ((cols_all, cols), (edges_all, edges), (before_all, before))
    loads = load_all(pairs, load_sem)
    ag = Courier(g, table, h, 2, send_sem, recv_sem)
    ag.own()[...] = node[...].astype(BF16)
    tally[...] = jnp.zeros_like(tally)
    total[...] = jnp.zeros_like(total)
    g.greet()
    wide = lambda ref: ref[layer : layer + 1, :]
    outs = (sent_out, pre_out, normed_out, update_out) + ((edges_out,) if first_layer else ())

    def meanwhile(at):
        if first_layer:
            tiles = place.shape[0]
            some = range(at * tiles // 3, (at + 1) * tiles // 3)
            find_places(rows, node_count, some, senders, receivers, live, place, side, joined.at[:, pl.ds(width, 128)], counts)
        if at == 0:
            for copy in loads:
                copy.wait()

        def cast_rows(i, carry):
            part = pl.ds(pl.multiple_of(i * 2 * group, 2 * group), 2 * group)
            joined[part, 0:width] = plain[part, :].astype(BF16)
            return carry

        lax.fori_loop(at * rows // 6, (at + 1) * rows // 6, cast_rows, 0)

    def leave(n, part):
        slot = lax.rem(n, 2)
        copies = [pltpu.make_async_copy(out_buf.at[slot, i], ref.at[part], out_sem.at[slot, i]) for i, ref in enumerate(outs)]
        return copies + [pltpu.make_async_copy(scale_buf.at[slot], scale_out.at[part], out_sem.at[slot, 5])]

    def spot(z, x):
        pair = g.block(z, x, 0)
        first = pl.multiple_of(pair * group, 2 * group)
        return pair, first, pl.ds(first, 2 * group)

    def moved_copy(z, x):
        part = spot(z, x)[2]
        return pltpu.make_async_copy(ordered.at[part], moved_out.at[part], moved_sem.at[z * g.X + x])

    def prepare(z, x):
        pair, first, part = spot(z, x)
        pick = picker(place, first, 2 * group)
        moved = dot(pick, joined[...])
        ordered[part, :] = moved[:, :width].astype(BF16)
        moved_copy(z, x).start()
        if first_layer:
            digits = moved[:, width:]
            lanes = lax.broadcasted_iota(jnp.int32, digits.shape, 1)
            ids = digits[:, 0:1] * 16.0 + digits[:, 1:2]
            got = digits[:, 2:3] * 16.0 + digits[:, 3:4]
            cols[part, :] = jnp.where(lanes == 0, ids, jnp.where(lanes == 1, got, jnp.where(lanes == 2, digits[:, 4:5], 0.0)))
            for half in range(2):
                digits = dot_nt(side[...], pick[half * group : (half + 1) * group])
                rows_of[pair + half] = jnp.concatenate(
                    [digits[0:1] * 16.0 + digits[1:2], digits[2:3] * 16.0 + digits[3:4], digits[4:10]], axis=0
                )

    def work(z, x, n):
        def own():
            here = table[pl.ds(pl.multiple_of(g.row * node_count, 16), node_count), :]
            cast[...] = dot(here, w1[2 * width :, :]).astype(BF16)
            block_out[...] = here

        pl.when(n == 0)(own)
        pair, first, part = spot(z, x)

        def free():
            for copy in leave(n, part):
                copy.wait()

        pl.when(n >= 2)(free)
        slot = lax.rem(n, 2)
        low = ordered[part, :] if first_layer else edges[part, :]
        cols_here = cols[part, :]
        send_pick = one_hot_cols(cols_here[:, 0:1], node_count)
        recv_pick = one_hot_cols(cols_here[:, 1:2], node_count)
        start = pl.multiple_of(pair * node_count, 16)
        sent = jnp.concatenate(
            [
                dot(send_pick[:group], table[pl.ds(start, node_count), :]).astype(BF16),
                dot(send_pick[group:], table[pl.ds(start + node_count, node_count), :]).astype(BF16),
            ],
            axis=0,
        )
        out_buf[slot, 0] = sent
        pre = dot(low, w1[:width, :]) + dot(sent, w1[width : 2 * width, :]) + dot(recv_pick, cast[...]) + wide(b1)
        out_buf[slot, 1] = pre.astype(BF16)
        active = (pre * lax.logistic(pre)).astype(BF16)
        normed, scale = norm_parts(dot(active, w2[...]) + wide(b2))
        out_buf[slot, 2] = normed.astype(BF16)
        scale_buf[slot] = jnp.broadcast_to(scale, (2 * group, 128))
        update = (normed * wide(gain) + wide(shift)) * cols_here[:, 2:3]
        update_low = update.astype(BF16)
        edge = low.astype(F32) + update
        if first_layer:
            out_buf[slot, 3] = update_low
            out_buf[slot, 4] = edge.astype(BF16)
        else:
            out_buf[slot, 3] = (before[part, :].astype(F32) + update).astype(BF16)
        tally[8:16, :] += fold(edge * edge)
        tally[16:24, :] += fold(update * update)
        for half in range(2):
            pick = one_hot_rows(rows_of[pair + half][1:2, :], node_count)
            total[...] += dot(pick, update_low[half * group : (half + 1) * group])
        for copy in leave(n, part):
            copy.start()

    ag.run(WORK_ORDER, meanwhile, prepare, work)
    copies = []
    for j in range(1, levels):
        l, l_dev = g.l_other(j)
        near[j - 1] = total[pl.ds(pl.multiple_of(l * h, h), h), :].astype(BF16)
        copy = pltpu.make_async_remote_copy(
            near.at[j - 1], far.at[levels - 1 - j], near_send.at[j - 1], near_recv.at[levels - 1 - j], device_id=l_dev, device_id_type=MESH
        )
        copy.start()
        copies.append(copy)
    received = total[pl.ds(pl.multiple_of(g.l * h, h), h), :]
    npre = dot(node[...].astype(BF16), nw1[:width, :]) + wide(nb1)
    for copy in copies:
        copy.wait()
    for j in range(1, levels):
        received = received + far[j - 1].astype(F32)
    received = received.astype(BF16)
    recv_out[...] = received
    npre = npre + dot(received, nw1[width:, :])
    npre_out[...] = npre
    nnormed, nscale = norm_parts(dot((npre * lax.logistic(npre)).astype(BF16), nw2[...]) + wide(nb2))
    nnormed_out[...] = nnormed
    nscale_out[...] = jnp.broadcast_to(nscale, (h, 128))
    change = nnormed * wide(ngain) + wide(nshift)
    new = node[...] + change
    node_out[...] = new
    tally[0:8, :] = fold(new * new)
    tally[24:32, :] = fold(change * change)
    for n in range(2):
        for copy in leave(n, pl.ds(0, 2 * group)):
            copy.wait()
    for n in range(4 * g.X):
        moved_copy(n // g.X, n % g.X).wait()
    ag.finish()


def forward_layer(layer, node, small, weights, plain, index, edges=None, before=None):
    levels, rows = lax.axis_size("lvl"), lax.axis_size("row")
    width = node.shape[1]
    h = node.shape[0] // (levels if layer == 0 else 1)
    count = plain.shape[0]
    group = count // rows
    vmem = pl.BlockSpec(memory_space=pltpu.VMEM)
    hbm = pl.BlockSpec(memory_space=pl.ANY)
    first_layer = layer == 0
    shape = jax.ShapeDtypeStruct
    wide = shape((count, width), BF16)
    ins = (node,) + small + weights + (plain,) + index
    in_specs = [vmem] * 9 + [hbm] * 5
    outs = [wide] * 5
    out_specs = [hbm] * 5
    scratch = []
    if first_layer:
        in_specs += [vmem, vmem, pl.BlockSpec(memory_space=pltpu.SMEM)]
        outs += [wide, shape(index[0].shape, jnp.int32), shape((rows, 8, group), F32), shape((count, 128), F32)]
        out_specs += [hbm, vmem, vmem, vmem]
        scratch = [pltpu.VMEM((16, count), BF16), pltpu.VMEM((rows, 128), F32)]
    else:
        ins += (edges, before)
        in_specs += [vmem, vmem, hbm, hbm, hbm]
        scratch = [pltpu.VMEM((count, 128), F32), pltpu.VMEM((count, width), BF16), pltpu.VMEM((count, width), BF16)]
    outs += [
        shape((count, 128), F32),
        shape((h * levels, width), BF16),
        shape((h, width), F32),
        shape((h, width), BF16),
        shape((h, width), F32),
        shape((h, width), F32),
        shape((h, 128), F32),
        shape((32, width), F32),
    ]
    out_specs += [hbm] + [vmem] * 7
    others = max(levels - 1, 1)
    return pl.pallas_call(
        functools.partial(forward_kernel, layer, levels, rows, first_layer),
        out_shape=outs,
        in_specs=in_specs,
        out_specs=out_specs,
        scratch_shapes=[
            pltpu.VMEM((rows * h * levels, width), BF16),
            pltpu.VMEM((h * levels, width), F32),
            pltpu.VMEM((h * levels, width), BF16),
            pltpu.VMEM((others, h, width), BF16),
            pltpu.VMEM((others, h, width), BF16),
        ]
        + [pltpu.VMEM(weight.shape[1:], BF16) for weight in weights]
        + [
            pltpu.VMEM((count, width), F32),
            pltpu.VMEM((count, width + (128 if first_layer else 0)), BF16),
            pltpu.VMEM((count, width), BF16),
            pltpu.VMEM((2, 5, 2 * group, width), BF16),
            pltpu.VMEM((2, 2 * group, 128), F32),
            pltpu.SemaphoreType.DMA((8,)),
            pltpu.SemaphoreType.DMA((2, 6)),
            pltpu.SemaphoreType.DMA((rows // 2,)),
            pltpu.SemaphoreType.DMA((Courier.sends(levels, rows, 2),)),
            pltpu.SemaphoreType.DMA((Courier.receives(levels, rows, 2),)),
            pltpu.SemaphoreType.DMA((others,)),
            pltpu.SemaphoreType.DMA((others,)),
        ]
        + scratch,
        compiler_params=pltpu.CompilerParams(collective_id=1 + layer, has_side_effects=True, vmem_limit_bytes=VMEM_BYTES),
        name=f"forward_{layer}",
    )(*ins)


def backward_kernel(
    layer, levels, rows, last_layer, share,
    d_node, block, recv, npre, nnormed, nscale, rows_of, gain, ngain, node, d_before, cols_all, scale_all, d_edges, pre, normed, edges, sent,
    w1_all, w2_all, nw1_all, nw2_all, other_grads,
    d_node_out, d_edges_out, d_change_out, grads, tally, node_all, other_out,
    stage, inbox, bufs, d_recv, turned, own_sum, out_buf, cols, scale, w1, w2, nw1, nw2,
    load_sem, out_sem, send_sem, recv_sem, near_send, near_recv, *more,
):
    g = Grid(levels, rows)
    h, width = d_node_out.shape
    if last_layer:
        d_node = d_node.at[pl.ds(pl.multiple_of(g.l * h, h), h)]
    count = pre.shape[0]
    group = count // rows
    node_count = h * levels
    loads = load_all(
        ((nw2_all.at[layer], nw2), (nw1_all.at[layer], nw1), (w1_all.at[layer], w1), (w2_all.at[layer], w2))
        + tuple((src, bufs.at[i]) for i, src in enumerate((d_edges, pre, normed, edges, sent)))
        + ((cols_all, cols), (scale_all, scale)),
        load_sem,
    )
    if share:
        other_stage, other_inbox, other_total, other_send, other_recv, other_sem = more
        other_load = pltpu.make_async_copy(other_grads, other_stage, other_sem)
        other_load.start()
        other = Scatter(g, other_stage, other_inbox, share, other_send, other_recv)
        early = other.steps // 2
    rs = Scatter(g, stage, inbox, h, send_sem, recv_sem)
    wide = lambda ref: ref[layer : layer + 1, :]
    mine = pl.ds(pl.multiple_of(g.l * h, h), h)
    own_sum[...] = jnp.zeros_like(own_sum)
    tally[...] = jnp.zeros_like(tally)
    for copy in loads[:2]:
        copy.wait()
    tally[48:56, :] = fold(d_node[...] * nnormed[...])
    tally[56:64, :] = fold(d_node[...])
    d_two = norm_back(nnormed[...], nscale[:, 0:1], d_node[...] * wide(ngain)).astype(BF16)
    tally[40:48, :] = fold(d_two.astype(F32))
    d_one = silu_back(npre[...], dot_nt(d_two, nw2[...])).astype(BF16)
    tally[32:40, :] = fold(d_one.astype(F32))
    d_recv[mine, :] = dot_nt(d_one, nw1[width:, :]).astype(BF16)
    g.greet()
    copies = []
    for j in range(1, levels):
        copy = pltpu.make_async_remote_copy(
            d_recv.at[mine], d_recv.at[mine], near_send.at[j - 1], near_recv.at[levels - 1 - j], device_id=g.l_other(j)[1], device_id_type=MESH
        )
        copy.start()
        copies.append(copy)
    d_node_out[...] = d_node[...] + dot_nt(d_one, nw1[:width, :])
    active = (npre[...] * lax.logistic(npre[...])).astype(BF16)
    grads[4 * width + width : 6 * width, :] = dot_tn(recv[...], d_one).astype(BF16)
    grads[4 * width : 5 * width, :] = dot_tn(block[mine, :], d_one).astype(BF16)
    grads[6 * width : 7 * width, :] = dot_tn(active, d_two).astype(BF16)
    if last_layer:
        node_all[mine, :] = node[...].astype(BF16)
    if share:
        other_load.wait()

        def first(m, carry):
            other.go(m, 2)
            return carry

        lax.fori_loop(0, early, first, 0)
    for copy in copies:
        copy.wait()
    copies = []
    for j in range(1, levels if last_layer else 1):
        copy = pltpu.make_async_remote_copy(
            node_all.at[mine],
            node_all.at[mine],
            near_send.at[levels + j - 2],
            near_recv.at[2 * levels - 2 - j],
            device_id=g.l_other(j)[1],
            device_id_type=MESH,
        )
        copy.start()
        copies.append(copy)
    for copy in loads[2:]:
        copy.wait()

    def work(i):
        z, x = rs.place(i)
        pair = g.block(z, x, 0)
        start = pl.multiple_of(pair * group, 2 * group)
        place = pl.ds(start, 2 * group)
        if not last_layer:
            earlier = pltpu.make_async_copy(d_before.at[place], out_buf.at[lax.rem(i, 2), 0], out_sem.at[lax.rem(i, 2), 0])
            earlier.start()
        cols_here = cols[place, :]
        recv_pick = one_hot_cols(cols_here[:, 1:2], node_count)
        d_edge = bufs[0, place, :].astype(F32)
        d_update = (d_edge + dot(recv_pick, d_recv[...])) * cols_here[:, 2:3]
        norm_here = bufs[2, place, :].astype(F32)
        tally[16:24, :] += fold(d_update * norm_here)
        tally[24:32, :] += fold(d_update)
        d_two = norm_back(norm_here, scale[place, 0:1], d_update * wide(gain)).astype(BF16)
        tally[8:16, :] += fold(d_two.astype(F32))
        pre_here = bufs[1, place, :].astype(F32)
        gate = lax.logistic(pre_here)
        d_one = (dot_nt(d_two, w2[...]) * (gate * (1.0 + pre_here * (1.0 - gate)))).astype(BF16)
        tally[0:8, :] += fold(d_one.astype(F32))
        bufs[0, place, :] = d_one
        bufs[1, place, :] = (pre_here * gate).astype(BF16)
        bufs[2, place, :] = d_two
        d_here = dot_nt(d_one, w1[:width, :])
        slot = lax.rem(i, 2)
        used = [
            pltpu.make_async_copy(out_buf.at[slot, n], ref.at[place], out_sem.at[slot, n])
            for n, ref in enumerate((d_edges_out, d_change_out))
            if n or last_layer
        ]

        def free():
            for copy in used:
                copy.wait()

        pl.when(i >= 2)(free)
        if last_layer:
            out_buf[slot, 0] = (d_edge + d_here).astype(BF16)
            out_buf[slot, 1] = d_here.astype(BF16)
        else:
            earlier.wait()
            out_buf[slot, 1] = (out_buf[slot, 0].astype(F32) + d_here).astype(BF16)
        for copy in used:
            copy.start()
        d_sent = dot_nt(d_one, w1[width : 2 * width, :]).astype(BF16)
        for half in range(2):
            ids = rows_of[pair + half]
            part = slice(half * group, (half + 1) * group)
            own_sum[...] += dot(one_hot_rows(ids[1:2, :], node_count), d_one[part])
            spot = pl.ds(pl.multiple_of((pair + half) * node_count, 16), node_count)
            stage[spot, :] = dot(one_hot_rows(ids[0:1, :], node_count), d_sent[part]).astype(BF16)

        def close():
            low = own_sum[...].astype(BF16)
            spot = pl.ds(pl.multiple_of(g.row * node_count, 16), node_count)
            stage[spot, :] = (stage[spot, :].astype(F32) + dot_nt(low, w1[2 * width :, :])).astype(BF16)
            grads[2 * width : 3 * width, :] = dot_tn(block[...], low).astype(BF16)

        pl.when(i == rs.blocks - 1)(close)

    def step(m):
        pl.when(m < rs.blocks)(lambda: work(m))
        for n, (at, left, right) in enumerate(((0, 3, 0), (1, 4, 0), (3, 1, 2))):

            def grad(at=at, left=left, right=right):
                grads[at * width : (at + 1) * width, :] = dot_tn(bufs[left], bufs[right]).astype(BF16)

            pl.when(m == rs.blocks + n)(grad)
        if share:
            pl.when(m + early < other.steps)(lambda: other.go(m + early, 2))

    rs.run(step)
    if share:
        other.ahead = 2
        other.last(other_total)
        other_out[...] = other_total[...].astype(BF16)
        other.finish()
    rs.last(turned)
    for copy in copies:
        copy.wait()
    d_node_out[...] += turned[...]
    for slot in range(2):
        for n, ref in enumerate((d_edges_out, d_change_out)):
            if n or last_layer:
                pltpu.make_async_copy(out_buf.at[slot, n], ref.at[pl.ds(0, 2 * group)], out_sem.at[slot, n]).wait()
    rs.finish()


def backward_layer(layer, last_layer, d_node, node_saved, cols, rows_of, scale, small, weights, d_edges, edge_saved, node, d_before, other_grads=None, share=0):
    levels, rows = lax.axis_size("lvl"), lax.axis_size("row")
    width = d_node.shape[1]
    h = d_node.shape[0] // (levels if last_layer else 1)
    count = d_edges.shape[0]
    group = count // rows
    vmem = pl.BlockSpec(memory_space=pltpu.VMEM)
    hbm = pl.BlockSpec(memory_space=pl.ANY)
    shape = jax.ShapeDtypeStruct
    ins = (d_node,) + node_saved + (rows_of,) + small + (node, d_before, cols, scale, d_edges) + edge_saved + weights
    ins += (other_grads if share else d_before,)
    outs = (
        shape((h, width), F32),
        shape((count, width) if last_layer else (16, 128), BF16),
        shape((count, width), BF16),
        shape((7 * width, width), BF16),
        shape((64, width), F32),
        shape((h * levels, width) if last_layer else (16, 128), BF16),
        shape((share, width) if share else (16, 128), BF16),
    )
    others = max(levels - 1, 1)
    return pl.pallas_call(
        functools.partial(backward_kernel, layer, levels, rows, last_layer, share),
        out_shape=outs,
        in_specs=[vmem] * (len(ins) - 13) + [hbm] * 13,
        out_specs=(vmem, hbm, hbm, vmem, vmem, vmem, vmem),
        scratch_shapes=[
            pltpu.VMEM((rows * h * levels, width), BF16),
            pltpu.VMEM((Scatter.receives(levels, rows), h, width), BF16),
            pltpu.VMEM((5, count, width), BF16),
            pltpu.VMEM((h * levels, width), BF16),
            pltpu.VMEM((h, width), F32),
            pltpu.VMEM((h * levels, width), F32),
            pltpu.VMEM((2, 2, 2 * group, width), BF16),
            pltpu.VMEM((count, 128), F32),
            pltpu.VMEM((count, 128), F32),
        ]
        + [pltpu.VMEM(weight.shape[1:], BF16) for weight in weights]
        + [
            pltpu.SemaphoreType.DMA((11,)),
            pltpu.SemaphoreType.DMA((2, 2)),
            pltpu.SemaphoreType.DMA((Scatter.sends(levels, rows),)),
            pltpu.SemaphoreType.DMA((2 * Scatter.receives(levels, rows),)),
            pltpu.SemaphoreType.DMA((2 * others,)),
            pltpu.SemaphoreType.DMA((2 * others,)),
                ]
        + (
            [
                pltpu.VMEM((share * levels * rows, width), BF16),
                pltpu.VMEM((Scatter.receives(levels, rows), share, width), BF16),
                pltpu.VMEM((share, width), F32),
                pltpu.SemaphoreType.DMA((Scatter.sends(levels, rows),)),
                pltpu.SemaphoreType.DMA((2 * Scatter.receives(levels, rows),)),
                pltpu.SemaphoreType.DMA,
            ]
            if share
            else []
        ),
        compiler_params=pltpu.CompilerParams(collective_id=3 + layer, has_side_effects=True, vmem_limit_bytes=VMEM_BYTES),
        name=f"backward_{layer}",
    )(*ins)


def sum_cuts(h):
    return 4 if h % 64 == 0 else 1


def sum_kernel(levels, rows, h, count, share, *refs):
    d_node, place, update, d_change, other_piece = refs[:5]
    terms = refs[5 : count + 5]
    (
        out, d_node_all, update_out, d_change_out, other_out, stage, inbox, total,
        scatter_send, scatter_recv, gather_send, gather_recv, load_sem, near_send, near_recv,
    ) = refs[count + 5 : count + 20]
    g = Grid(levels, rows)
    mine = pl.ds(pl.multiple_of(g.l * d_node.shape[0], d_node.shape[0]), d_node.shape[0])
    d_node_all[mine, :] = d_node[...].astype(BF16)
    pairs = []
    at = 0
    for term in terms:
        pairs.append((term, stage.at[pl.ds(at, term.shape[0])]))
        at += term.shape[0]
    loads = load_all(pairs, load_sem)
    g.greet()
    for copy in loads:
        copy.wait()
    copies = []
    for j in range(1, levels):
        copy = pltpu.make_async_remote_copy(
            d_node_all.at[mine], d_node_all.at[mine], near_send.at[j - 1], near_recv.at[levels - 1 - j], device_id=g.l_other(j)[1], device_id_type=MESH
        )
        copy.start()
        copies.append(copy)
    tiles = place.shape[0]
    size = 256 if tiles % 2 == 0 else 128
    lane = lax.broadcasted_iota(jnp.int32, (128, 128), 1).astype(F32)

    def restore(i):
        pick = []
        for part in range(size // 128):
            spot = jnp.broadcast_to(place[pl.ds(i * (size // 128) + part, 1), :], (128, 128)).astype(F32).T
            pick.append(jnp.concatenate([(spot == lane + float(128 * j)).astype(BF16) for j in range(tiles)], axis=1))
        pick = jnp.concatenate(pick, axis=0)
        here = pl.ds(pl.multiple_of(i * size, size), size)
        update_out[here, :] = dot(pick, update[...]).astype(BF16)
        d_change_out[here, :] = dot(pick, d_change[...]).astype(BF16)

    rs = Scatter(g, stage, inbox, h, scatter_send, scatter_recv)
    after = tiles * 128 // size

    if share:
        other = Gather(g, other_out, share, *refs[count + 20 :])
        other.slot(g.row, g.l)[...] = other_piece[...]
        other.begin()

    def work(m):
        pl.when(m < after)(lambda: restore(jnp.minimum(m, after - 1)))
        if share:
            for s in range(2):
                pl.when((lax.rem(m, 2) == s) & (m < 14))(lambda s=s: other.wave(m // 2, s))

    rs.run(work, ahead=2, steps=max(rs.steps, 14))

    def more(i, carry):
        restore(i)
        return carry

    if after > rs.steps:
        lax.fori_loop(rs.steps, after, more, 0)
    rs.last(total)
    ag = Courier(g, out, h, sum_cuts(h), gather_send, gather_recv)
    ag.own()[...] = total[...].astype(BF16)
    ag.run(ORDER if ag.cuts == 4 else PLAIN_ORDER)
    for copy in copies:
        copy.wait()
    rs.finish()
    if share:

        def last_waits(i, carry):
            other.mates(i // g.X, lax.rem(i, g.X))
            return carry

        lax.fori_loop(0, 4 * g.X, last_waits, 0)
        other.finish()
    ag.finish()


def sum_pieces(d_node, place, update, d_change, other_piece, terms, call, share):
    levels, rows = lax.axis_size("lvl"), lax.axis_size("row")
    width = terms[0].shape[1]
    count = sum(term.shape[0] for term in terms)
    h = count // (levels * rows)
    vmem = pl.BlockSpec(memory_space=pltpu.VMEM)
    shape = jax.ShapeDtypeStruct
    return pl.pallas_call(
        functools.partial(sum_kernel, levels, rows, h, len(terms), share),
        out_shape=(
            shape((count, width), BF16),
            shape((d_node.shape[0] * levels, width), BF16),
            shape(update.shape, BF16),
            shape(update.shape, BF16),
            shape((share * levels * rows, width) if share else (16, 128), BF16),
        ),
        in_specs=[vmem] * 5 + [pl.BlockSpec(memory_space=pl.ANY)] * len(terms),
        out_specs=(vmem,) * 5,
        scratch_shapes=[
            pltpu.VMEM((count, width), BF16),
            pltpu.VMEM((Scatter.receives(levels, rows), h, width), BF16),
            pltpu.VMEM((h, width), F32),
            pltpu.SemaphoreType.DMA((Scatter.sends(levels, rows),)),
            pltpu.SemaphoreType.DMA((2 * Scatter.receives(levels, rows),)),
            pltpu.SemaphoreType.DMA((Courier.sends(levels, rows, sum_cuts(h)),)),
            pltpu.SemaphoreType.DMA((Courier.receives(levels, rows, sum_cuts(h)),)),
            pltpu.SemaphoreType.DMA((len(terms),)),
            pltpu.SemaphoreType.DMA((max(levels - 1, 1),)),
            pltpu.SemaphoreType.DMA((max(levels - 1, 1),)),
        ]
        + ([pltpu.SemaphoreType.DMA((Gather.sends(levels, rows),)), pltpu.SemaphoreType.DMA((2 * rows * levels,))] if share else []),
        compiler_params=pltpu.CompilerParams(collective_id=call, has_side_effects=True, vmem_limit_bytes=VMEM_BYTES),
        name=f"sum_{call}",
    )(d_node, place, update, d_change, other_piece, *terms)


def finish_kernel(parts, smalls, update, d_change, first_sums, last_sums, node, d_node, edges, cot, edge_out, cot_out, *refs):
    count = len(parts) + smalls
    wide_outs, small_outs = refs[: len(parts)], refs[len(parts) : count]
    rms_out, node_out, d_node_out, sums, rest, lows, ins, outs, wide, sums_sem, low_sem, in_sem, out_sem, wide_sem = refs[count:]
    size, width = ins.shape[2:]
    steps = edges.shape[0] // size
    targets = [(n, i) for n, part in enumerate(parts) for i in range(part)]
    big = sums.shape[1]
    loads = load_all([(ref.at[pl.ds(0, big)], sums.at[layer]) for layer, ref in enumerate((first_sums, last_sums))], sums_sem)
    loads.append(pltpu.make_async_copy(first_sums.at[pl.ds(big, rest.shape[0])], rest, low_sem.at[4]))
    loads[-1].start()

    def load(step):
        here = pl.ds(step * size, size)
        pairs = ((edges, ins.at[step % 2, 0], in_sem.at[step % 2, 0]), (cot, ins.at[step % 2, 1], in_sem.at[step % 2, 1]))
        pairs += ((update, lows.at[step % 2, 0], low_sem.at[step % 2 * 2]), (d_change, lows.at[step % 2, 1], low_sem.at[step % 2 * 2 + 1]))
        return [pltpu.make_async_copy(ref.at[here], to, sem) for ref, to, sem in pairs]

    def leave(step):
        here = pl.ds(step * size, size)
        return [pltpu.make_async_copy(outs.at[step % 2, n], ref.at[here], out_sem.at[step % 2, n]) for n, ref in enumerate((edge_out, cot_out))]

    def widen(at):
        n, i = targets[at % len(targets)]
        ref = wide_outs[n].at[at // len(targets), pl.ds(i * width, width)]
        return pltpu.make_async_copy(wide.at[at % 4], ref, wide_sem.at[at % 4])

    total = 2 * len(targets)
    done = 0
    for copy in load(0):
        copy.start()
    for step in range(steps):
        if step + 1 < steps:
            for copy in load(step + 1):
                copy.start()
        for copy in load(step):
            copy.wait()
        if step >= 2:
            for copy in leave(step - 2):
                copy.wait()
        for n in range(2):
            outs[step % 2, n] = ins[step % 2, n] + lows[step % 2, n].astype(F32)
        for copy in leave(step):
            copy.start()
        if step == 0:
            for copy in loads:
                copy.wait()
        while done < total * (step + 1) // steps:
            if done >= 4:
                widen(done - 4).wait()
            layer, at = done // len(targets), done % len(targets)
            wide[done % 4] = sums[layer, at * width : (at + 1) * width, :].astype(F32)
            widen(done).start()
            done += 1
    few = rest[...].astype(F32)
    for n, out in enumerate(small_outs):
        for layer in range(2):
            out[layer : layer + 1, :] = few[layer * smalls + n : layer * smalls + n + 1]
    rms_out[...] = few[2 * smalls : 2 * smalls + 1]
    node_out[...] = node[...].astype(F32)
    d_node_out[...] = d_node[...].astype(F32)
    for step in range(max(steps - 2, 0), steps):
        for copy in leave(step):
            copy.wait()
    for at in range(total - 4, total):
        widen(at).wait()


def finish_all(update, d_change, first_sums, last_sums, node, d_node, edges, cot, parts, smalls):
    count, width = edges.shape
    size = 512 if count % 512 == 0 else 128
    vmem = pl.BlockSpec(memory_space=pltpu.VMEM)
    hbm = pl.BlockSpec(memory_space=pl.ANY)
    shape = jax.ShapeDtypeStruct
    wide = (shape((count, width), F32),) * 2 + tuple(shape((2, part * width, width), F32) for part in parts)
    narrow = (shape((2, width), F32),) * smalls + (shape((1, width), F32), shape(node.shape, F32), shape(node.shape, F32))
    return pl.pallas_call(
        functools.partial(finish_kernel, parts, smalls),
        out_shape=wide + narrow,
        in_specs=[hbm] * 4 + [vmem] * 2 + [hbm] * 2,
        out_specs=(hbm,) * len(wide) + (vmem,) * len(narrow),
        scratch_shapes=[
            pltpu.VMEM((2, sum(parts) * width, width), BF16),
            pltpu.VMEM((32, width), BF16),
            pltpu.VMEM((2, 2, size, width), BF16),
            pltpu.VMEM((2, 2, size, width), F32),
            pltpu.VMEM((2, 2, size, width), F32),
            pltpu.VMEM((4, width, width), F32),
            pltpu.SemaphoreType.DMA((2,)),
            pltpu.SemaphoreType.DMA((5,)),
            pltpu.SemaphoreType.DMA((2, 2)),
            pltpu.SemaphoreType.DMA((2, 2)),
            pltpu.SemaphoreType.DMA((4,)),
        ],
        compiler_params=pltpu.CompilerParams(vmem_limit_bytes=VMEM_BYTES),
        name="finish_all",
    )(update, d_change, first_sums, last_sums, node, d_node, edges, cot)


def on_device(
    node_latent, edge_latent, senders, receivers, live_edges,
    edge_w1, edge_b1, edge_w2, edge_b2, edge_gain, edge_shift, node_w1, node_b1, node_w2, node_b2, node_gain, node_shift,
    node_cotangent, edge_cotangent,
):
    node_count, width = node_latent.shape
    edge_count = edge_latent.shape[0]
    layers = edge_w1.shape[0]
    row_total, level_total = lax.axis_size("row"), lax.axis_size("lvl")
    node = node_latent
    weights = (edge_w1, edge_w2, node_w1, node_w2)
    small = (edge_b1, edge_b2, edge_gain, edge_shift, node_b1, node_b2, node_gain, node_shift)
    tiles = edge_count // 128
    index = (senders.reshape(tiles, 128), receivers.reshape(tiles, 128), live_edges.reshape(1, 1))
    sent, pre, normed, update, edges, edges_next, place, rows_of, cols, scale, block, node, recv, npre, nnormed, nscale, tally = forward_layer(
        0, node, small, weights, edge_latent, index
    )
    first = ((block, recv, npre, nnormed, nscale), scale, (pre, normed, edges, sent))
    sent, pre, normed, update, d_edges, scale, block, node, recv, npre, nnormed, nscale, tally_last = forward_layer(
        1, node, small, weights, edge_cotangent, (place, rows_of, cols), edges_next, update
    )
    last = ((block, recv, npre, nnormed, nscale), scale, (pre, normed, edges_next, sent))
    tallies = [tally, tally_last]
    d_node = node_cotangent
    gains = (edge_gain, node_gain)
    devices = row_total * level_total
    even = 7 * width % (16 * devices) == 0 and devices <= 32
    share = 7 * width // devices if even else 0
    d_node, d_edges, d_change, last_grads, last_sums, node_all, _ = backward_layer(
        1, True, d_node, last[0], cols, rows_of, last[1], gains, weights, d_edges, last[2], node, d_edges
    )
    if not share:
        last_grads = lax.psum(last_grads, ("lvl", "row"))
    d_node, _, d_change, first_grads, first_sums, _, piece = backward_layer(
        0, False, d_node, first[0], cols, rows_of, first[1], gains, weights, d_edges, first[2], node, d_change, last_grads, share
    )
    sums = [first_sums, last_sums]
    small = jnp.concatenate([jnp.sum(part.reshape(8, 8, width), axis=1) for part in sums])
    squares = jnp.stack([jnp.sum(tally.reshape(4, 8 * width), axis=1) for tally in tallies])
    squares = jnp.pad(squares.reshape(1, -1), ((0, 0), (0, width - squares.size)))
    used = 7 * width + small.shape[0] + 1
    each = -(-used // (16 * devices)) * 16
    rest = [small.astype(BF16), squares.astype(BF16), jnp.zeros((each * devices - used, width), BF16)]
    flat, d_node_all, update, d_change, whole = sum_pieces(
        d_node, place, update, d_change, piece, [first_grads, jnp.concatenate(rest)], 5, share
    )
    last_grads = whole if share else last_grads
    edge_out, edge_grad, w1, w2, nw1, nw2, b1, b2, gain, shift, nb1, nb2, ngain, nshift, squares, node, d_node = finish_all(
        update, d_change, flat, last_grads, node_all, d_node_all, edge_latent, edge_cotangent, (3, 1, 2, 1), 8
    )
    node_entries = float(node_count * row_total * width)
    edge_entries = float(edge_count * row_total * level_total * width)
    entries = jnp.array([node_entries, edge_entries, edge_entries, node_entries], F32)
    rms = jnp.sqrt(squares[0, : 4 * layers].reshape(layers, 4) / entries[None, :])
    return node, edge_out, d_node, edge_grad, w1, b1, w2, b2, gain, shift, nw1, nb1, nw2, nb2, ngain, nshift, rms


def solution(mesh):
    rows, both, whole = P("row", None), P(("lvl", "row"), None), P()
    edge = P(("lvl", "row"))
    placed = (rows, both, edge, edge, edge) + (whole,) * 12 + (rows, both)
    outs = (rows, both, rows, both) + (whole,) * 13
    return jax.shard_map(on_device, mesh=mesh, in_specs=placed, out_specs=outs, check_vma=False)
```

profile of v0, /device:TPU:0, one launch (start us, length us, event | category | flops | bytes accessed | tf_op | source)
XLA Modules:
  0.0 384.3 jit_solution(15006297049164914575)
XLA Ops:
  1.3 0.1 pad.9.clone
  1.4 65.1 %forward_0.1 = (bf16[2560,512]{1,0:T(8,128)(2,1)}, bf16[2560,512]{1,0:T(8,128)(2,1)}, bf16[2560,512]{1,0:T(8,128)(2,1)}, bf16[2560,512]{1,0:T(8,128)(2,1)}, bf16...) custom-call(f32[512,512]{1,0:T(8,128)} %refs_0_.1, ...), custom_call_target="tpu_custom_call" | custom-call | tf_op jit(solution)/shard_map/forward_0/pallas_call | solution.py:1063
  66.5 1.0 reduce_sum.52
  67.4 0.1 reduce_sum.53
  67.5 0.1 reduce_sum.54
  67.6 57.0 %forward_1.1 = (bf16[2560,512]{1,0:T(8,128)(2,1)}, bf16[2560,512]{1,0:T(8,128)(2,1)}, bf16[2560,512]{1,0:T(8,128)(2,1)}, bf16[2560,512]{1,0:T(8,128)(2,1)}, bf16...) custom-call(f32[256,512]{1,0:T(8,128)} %get-tuple-element.80.refs_0_, ...), custom_call_target="tpu_custom_call" | custom-call | tf_op jit(solution)/shard_map/forward_1/pallas_call | solution.py:1063
  124.6 68.9 %backward_1.1 = (f32[256,512]{1,0:T(8,128)}, bf16[2560,512]{1,0:T(8,128)(2,1)}, bf16[2560,512]{1,0:T(8,128)(2,1)}, bf16[3584,512]{1,0:T(8,128)(2,1)}, f32[64,512...) custom-call(f32[512,512]{1,0:T(8,128)} %d_node.1, bf16[512,512]{1,0:T(8,128)(2,1)} %get-tuple-element.86.block, ...), custom_call_target="tpu_custom_call" | custom-call | tf_op jit(solution)/shard_map/backward_1/pallas_call | solution.py:1287
  193.5 0.0 copy-start
  193.5 0.0 copy-start.1
  193.6 81.7 %backward_0.1 = (f32[256,512]{1,0:T(8,128)}, bf16[16,128]{1,0:T(8,128)(2,1)}, bf16[2560,512]{1,0:T(8,128)(2,1)}, bf16[3584,512]{1,0:T(8,128)(2,1)}, f32[64,512]{...) custom-call(f32[256,512]{1,0:T(8,128)} %get-tuple-element.97.d_node, ...), custom_call_target="tpu_custom_call" | custom-call | tf_op jit(solution)/shard_map/backward_0/pallas_call | solution.py:1287
  275.2 0.0 copy-done
  275.2 1.0 bitcast_reduce_fusion
  276.2 0.0 copy-done.1
  276.2 0.1 reduce_sum.55
  276.3 0.1 reduce_sum.56
  276.4 0.1 reduce_sum.57
  276.6 0.1 reshape.63
  276.6 0.9 fusion.3.refs_6_
  277.6 84.9 %sum_5.1 = (bf16[4096,512]{1,0:T(8,128)(2,1)}, bf16[512,512]{1,0:T(8,128)(2,1)}, bf16[2560,512]{1,0:T(8,128)(2,1)}, bf16[2560,512]{1,0:T(8,128)(2,1)}, bf16[3584,512]{1,0:T(8,128)(2,1)}) custom-call(f32[256,512]{1,0:T(8,128)} %get-tuple-element.111.refs_0_, s32[20,128]{1,0:T(8,128)} %get-tuple-element.81.refs_14_.refs_1_, ...), custom_call_target="tpu_custom_call" | custom-call | tf_op jit(solution)/shard_map/sum_5/pallas_call | solution.py:1420
  362.5 0.0 copy-start.2
  362.5 20.2 %finish_all.1 = (f32[2560,512]{1,0:T(8,128)}, f32[2560,512]{1,0:T(8,128)}, f32[2,1536,512]{2,1,0:T(8,128)}, f32[2,512,512]{2,1,0:T(8,128)}, f32[2,1024,512]{2,1,...) custom-call(bf16[2560,512]{1,0:T(8,128)(2,1)} %get-tuple-element.120, ...), custom_call_target="tpu_custom_call" | custom-call | tf_op jit(solution)/shard_map/finish_all/pallas_call | solution.py:1525
  382.7 0.7 slice_reduce_fusion
  383.3 0.1 reshape_squeeze.3
  383.4 0.0 copy-done.2
  383.4 0.6 multiply_sqrt_fusion
  (2 shorter events, 0.0 us)
Async XLA Ops:
  193.5 81.7 %copy-start = (f32[64,512]{1,0:T(8,128)S(1)}, f32[64,512]{1,0:T(8,128)}, u32[]{:S(2)}) copy-start(f32[64,512]{1,0:T(8,128)} %get-tuple-element.117) | copy-start | bytes 393220
  193.5 82.7 %copy-start.1 = (f32[32,512]{1,0:T(8,128)S(1)}, f32[32,512]{1,0:T(8,128)}, u32[]{:S(2)}) copy-start(f32[32,512]{1,0:T(8,128)} %get-tuple-element.119) | copy-start | bytes 196612
  362.5 20.9 %copy-start.2 = (f32[4]{0:T(128)S(1)}, f32[4]{0:T(128)}, u32[]{:S(2)}) copy-start(f32[4]{0:T(128)} %constant.13) | copy-start | bytes 52
where the time goes:
time: 391 us; the launch traced here: 384 us
  Pallas kernels  378 us (97%)
    pallas_call x2, Pallas kernels, backward_layer(): pl.pallas_call(functools.partial(backward_kernel, layer, levels, rows, la...  151 us
    pallas_call x2, Pallas kernels, forward_layer(): pl.pallas_call(functools.partial(forward_kernel, layer, levels, rows, fir...  122 us
    pallas_call x1, Pallas kernels, sum_pieces(): pl.pallas_call(functools.partial(sum_kernel, levels, rows, h, len(terms),...  84.9 us
    pallas_call x1, Pallas kernels, finish_all(): pl.pallas_call(functools.partial(finish_kernel, parts, smalls), out_shape...  20.2 us

commit v1 on v0

--- a/solution.py
+++ b/solution.py
@@ -26,12 +26,12 @@
 )
 ORDER = (
     (
-        266400, 82449, 788882, 135431, 104611, 150052, 820491, 853654, 609459, 445454,
-        201638, 755629, 347034, 923038, 693433, 481974, 464424, 513978, 908990, 974399,
+        280580, 295586, 590612, 803888, 167948, 151730, 217752, 235036, 693301, 365337,
+        855736, 760990, 986429, 740022, 679230,
     ),
     (
-        4616, 168577, 183049, 854950, 200706, 541080, 645773, 661524, 559118, 804778,
-        281910, 940344, 414866, 774588, 1006515, 495253, 1018298, 1036204, 744878, 445995,
+        589832, 607380, 32934, 214538, 233524, 808981, 412469, 678712, 548394, 269996,
+        657586, 741656, 1023289, 464658, 479002,
     ),
 )
 PLAIN_ORDER = (
@@ -40,6 +40,27 @@
     ),
     (
         328704, 526372, 658444, 464948, 990252,
+    ),
+)
+
+TERMS_ORDER = (
+    (
+        246535, 230038, 329348, 54046, 34332, 180388, 147502, 722962, 432138, 820258,
+        692248, 2097073,
+    ),
+    (
+        115332, 247427, 184844, 19218, 328838, 233232, 463616, 397320, 431874, 558380,
+        825512, 2097072,
+    ),
+)
+SUM_ORDER = (
+    (
+        82311, 251910, 65686, 820894, 329484, 902566, 809372, 917796, 300826, 1162,
+        562704, 525336, 890169, 2087477,
+    ),
+    (
+        792839, 83844, 884894, 803212, 212998, 591254, 296090, 40115, 329752, 135950,
+        525623, 871970, 661038, 2087480,
     ),
 )
 
@@ -124,164 +145,6 @@
 def cuts(h):
     first = -(-h // 32) * 16
     return ((0, first), (first, h - first)) if h > first else ((0, h),)
-
-
-class Gather:
-    def __init__(self, grid, table, h, send_sem, recv_sem):
-        self.g, self.table, self.h = grid, table, h
-        self.cuts = cuts(h)
-        self.send_sem, self.recv_sem = send_sem, recv_sem
-        X, L = grid.X, grid.L
-        self.per_column = X + L + 1
-        self.per_sides = 2 * (X - 1) * (L - 1) + X - 1 + L - 1
-        self.at_sides = 4 * self.per_column
-        self.at_corners = self.at_sides + 4 * self.per_sides
-        self.drain = False
-
-    @staticmethod
-    def sends(levels, rows):
-        X, L = rows // 8, levels
-        return 2 * (4 * (X + L + 1) + 4 * (2 * (X - 1) * (L - 1) + X + L - 2) + 8 * (X - 1) * (L - 1))
-
-    def slot(self, block, l, s=None):
-        start, size = (0, self.h) if s is None else self.cuts[s]
-        return self.table.at[pl.ds(pl.multiple_of((block * self.g.L + l) * self.h + start, 16), size)]
-
-    def push(self, at, block, l, s, who, when=None):
-        place = self.slot(block, l, s)
-        copy = pltpu.make_async_remote_copy(
-            place, place, self.send_sem.at[2 * at + s], self.recv_sem.at[(block * self.g.L + l) * 2 + s], device_id=who, device_id_type=MESH
-        )
-        only(when, copy.wait_send if self.drain else copy.start)
-
-    def arrived(self, block, l, s):
-        if self.drain:
-            return
-        place = self.slot(block, l, s)
-        pltpu.make_async_remote_copy(
-            place, place, self.send_sem.at[0], self.recv_sem.at[(block * self.g.L + l) * 2 + s], device_id=self.g.mate(), device_id_type=MESH
-        ).wait_recv()
-
-    def column(self, k, s, own=False):
-        g = self.g
-        zk = g.nth(k)
-        block = g.block(zk, g.x, g.core)
-        at = k * self.per_column
-        if not own:
-            self.arrived(block, g.l, s)
-        self.push(at, block, g.l, s, g.at_z(g.z + 1), g.up & (zk <= g.z))
-        self.push(at + 1, block, g.l, s, g.at_z(g.z - 1), g.down & (zk >= g.z))
-        for i in range(1, g.X):
-            self.push(at + 1 + i, block, g.l, s, g.x_other(i)[1])
-        for j in range(1, g.L):
-            self.push(at + g.X + j, block, g.l, s, g.l_other(j)[1])
-        self.push(at + g.X + g.L, block, g.l, s, g.mate())
-
-    def sides(self, k, s):
-        g = self.g
-        zk = g.nth(k)
-        even = lax.rem(zk, 2) == 0
-        at = self.at_sides + k * self.per_sides
-        for i in range(1, g.X):
-            block = g.block(zk, g.x_other(i)[0], g.core)
-            self.arrived(block, g.l, s)
-            for j in range(1, g.L):
-                self.push(at, block, g.l, s, g.l_other(j)[1], g.local(zk) & even)
-                at = at + 1
-            self.push(at, block, g.l, s, g.mate())
-            at = at + 1
-        for j in range(1, g.L):
-            block = g.block(zk, g.x, g.core)
-            l = g.l_other(j)[0]
-            self.arrived(block, l, s)
-            for i in range(1, g.X):
-                self.push(at, block, l, s, g.x_other(i)[1], g.local(zk) & jnp.logical_not(even))
-                at = at + 1
-            self.push(at, block, l, s, g.mate())
-            at = at + 1
-
-    def corners(self, z, s, local):
-        g = self.g
-        q = lax.rem(z, 2) + (0 if local else 2)
-        for i in range(1, g.X):
-            block = g.block(z, lax.rem(g.x + i, g.X), g.core)
-            for j in range(1, g.L):
-                l = g.l_other(j)[0]
-                at = self.at_corners + ((q * (g.X - 1) + i - 1) * (g.L - 1) + j - 1) * 2
-                self.arrived(block, l, s)
-                if local:
-                    self.push(at, block, l, s, g.at_z(g.pair_z()))
-                self.push(at + 1, block, l, s, g.mate())
-
-    def mates(self, z, x):
-        for l in range(self.g.L):
-            for s in range(len(self.cuts)):
-                self.arrived(self.g.block(z, x, 1 - self.g.core), l, s)
-
-    def begin(self):
-        for s in range(len(self.cuts)):
-            self.column(0, s, own=True)
-
-    def wave(self, k, s):
-        g = self.g
-        pl.when(k < 3)(lambda: self.column(k + 1, s))
-        pl.when(k < 4)(lambda: self.sides(k, s))
-        if g.L == 1:
-            return
-        two = len(self.cuts) == 2
-        late = 1 - s if two else s
-        back = 2 - s if two else 1
-        for local, lag in ((True, back), (False, back + 1)):
-            who = None if local else g.pair_z()
-            kk = k - lag
-            z = g.nth(jnp.clip(kk, 0, 3), who)
-            pl.when((kk >= 0) & (kk < 4) & g.local(z, who))(lambda z=z, local=local: self.corners(z, late, local))
-
-    def due(self, k, c):
-        g = self.g
-        own = c == 0
-        far = c > g.X - 1
-        off = jnp.where(own, 0, lax.rem(c - 1, max(g.X - 1, 1)) + 1)
-        kk = jnp.where(own, k - 1, jnp.where(far, k - 3, k - 2))
-        who = jnp.where(far, g.pair_z(), g.z)
-        z = g.nth(jnp.clip(kk, 0, 3), who)
-        there = (kk >= 0) & (kk < 4) & (own | g.local(z, who))
-        return z, lax.rem(g.x + off, g.X), there
-
-    def run(self, work=None, meanwhile=None):
-        g = self.g
-        parts = 2 * g.X - 1
-        self.begin()
-
-        def one(i, done):
-            k, c = i // parts, lax.rem(i, parts)
-            for s in range(len(self.cuts)):
-                pl.when(c == s)(lambda s=s: self.wave(k, s))
-            if meanwhile is not None:
-                for at in range(3):
-                    pl.when(i == at)(lambda at=at: meanwhile(at))
-            z, x, there = self.due(k, c)
-
-            def ready():
-                self.mates(z, x)
-                if work is not None:
-                    work(z, x, done)
-
-            pl.when(there)(ready)
-            return done + there.astype(jnp.int32)
-
-        lax.fori_loop(0, 7 * parts, one, jnp.int32(0))
-
-    def finish(self):
-        self.drain = True
-        self.begin()
-
-        def one(k, carry):
-            for s in range(len(self.cuts)):
-                self.wave(k, s)
-            return carry
-
-        lax.fori_loop(0, 7, one, 0)
 
 
 class Courier:
@@ -488,7 +351,6 @@
             self.out[name] = at
             at += count
         self.drain = False
-        self.prepare()
 
     @staticmethod
     def parts(X, L):
@@ -578,7 +440,7 @@
         g = self.g
         x, x_dev = g.x_other(i)
         block = g.block(z, x, g.core)
-        even = lax.rem(z, 2) == 0
+        even = self.even(z)
         side = (g.X - 1) * (g.L - 1)
         for j in range(1, g.L):
             l, l_dev = g.l_other(j)
@@ -639,96 +501,54 @@
 
                 pl.when(there)(take)
 
-    @staticmethod
-    def plan(X, hop=2):
-        orders, spots = [], []
-        for z in range(4):
-            corners = (3, 2, 1, 0) if z < 2 else (0, 1, 2, 3)
-            own = tuple(reversed(NEAREST[z]))
-            order = []
-            for j in range(4):
-                order += [(corners[j], off) for off in range(1, X)] + [(own[j], 0)]
-            orders.append(order)
-            spots.append(({zk: max(m for m, (a, off) in enumerate(order) if a == zk and off) for zk in range(4)},
-                          {zk: order.index((zk, 0)) for zk in range(4)}))
-        names = ("far", "sx", "sl", "near", "sx_late", "sl_late", "column")
-        due = [{name: {} for name in names} for _ in range(4)]
-
-        def put(z, name, zk, step):
-            while step in due[z][name]:
-                step += 1
-            due[z][name][step] = zk
-            return step
-
-        sides = [{}, {}, {}, {}]
-        for z in range(4):
-            pair = z + 1 - 2 * (z % 2)
-            for zk in sorted(range(4), key=lambda a: spots[z][0][a]):
-                near = zk // 2 == z % 2
-                corner, own = spots[z][0][zk] + 1, spots[z][1][zk] + 1
-                ready = put(z, "near", zk, max(corner, spots[pair][0][zk] + 1 + hop)) if near else put(z, "far", zk, corner)
-                sx = put(z, "sx_late", zk, ready + hop) if near and zk % 2 == 0 else put(z, "sx", zk, corner)
-                sl = put(z, "sl_late", zk, max(ready + hop, own)) if near and zk % 2 else put(z, "sl", zk, own)
-                sides[z][zk] = max(sx, sl)
-        for zk in range(4):
-            for chain in (range(0, zk), range(3, zk, -1)):
-                before = 0
-                for z in chain:
-                    before = put(z, "column", zk, max(sides[z][zk], before) + hop)
-        steps = 1 + max(step for z in range(4) for name in names for step in due[z][name])
-        return orders, due, steps
-
-    def prepare(self):
-        self.orders, self.due, self.steps = self.plan(self.g.X)
-        self.blocks = 4 * self.g.X
-
-    def pick(self, tables, m):
-        out = jnp.int32(-1)
-        for z in range(4):
-            for at, value in tables[z].items():
-                out = jnp.where((self.g.z == z) & (m == at), value, out)
-        return out
-
-    def place(self, m):
-        g = self.g
-        code = self.pick([{at: zk * g.X + off for at, (zk, off) in enumerate(order)} for order in self.orders], m)
-        return code // g.X, lax.rem(g.x + lax.rem(code, g.X), g.X)
-
-    def step(self, m):
-        g = self.g
-
-        def first():
-            self.to_mate(*self.place(m))
-
-        def second():
-            self.from_mate(*self.place(m - 1))
-
-        pl.when(m < self.blocks)(first)
-        pl.when((m >= 1) & (m <= self.blocks))(second)
-
-        def send(name, act, over_x):
-            zk = self.pick([due[name] for due in self.due], m)
-
-            def go():
-                if over_x:
-                    for i in range(1, g.X):
-                        act(zk, i)
-                else:
-                    act(zk)
-
-            pl.when(zk >= 0)(go)
-
-        send("column", self.column, False)
-        send("sl_late", lambda zk: self.side_l(zk, True), False)
-        send("sx_late", lambda zk, i: self.side_x(zk, i, True), True)
+    def even(self, zk):
+        return lax.rem(jnp.where(self.g.z < 2, zk, 3 - zk), 2) == 0
+
+    def decode(self, m):
+        g = self.g
+        first = (g.z == 0) | (g.z == 3)
+        word = jnp.int32(0)
+        for at, (a, b) in enumerate(zip(*self.tables)):
+            word = jnp.where(m // 3 == at, jnp.where(first, a, b), word)
+        byte = lax.rem(m, 3)
+        code = lax.rem(jnp.where(byte == 0, word, jnp.where(byte == 1, word // 128, word // 16384)), 128)
+        zk = lax.rem(code // 2, 4)
+        return code, code // 8, jnp.where(g.z < 2, zk, 3 - zk), lax.rem(code, 2)
+
+    def step(self, m, work=None, extra=None, done=0):
+        g = self.g
+        code, kind, zk, side = self.decode(m)
+        for off in range(g.X):
+            x = lax.rem(g.x + off, g.X)
+            hit = side == (0 if off == 0 else 1)
+
+            def make(x=x, off=off):
+                if work is not None and not self.drain:
+                    work(zk, x, done + max(off - 1, 0))
+                self.to_mate(zk, x)
+
+            pl.when((kind == 0) & hit)(make)
+            if not self.drain:
+                pl.when((kind == 1) & hit)(lambda x=x: self.from_mate(zk, x))
+        near = g.local(zk)
+        for i in range(1, g.X):
+            if g.L > 1:
+                pl.when((kind == 2) & near)(lambda i=i: self.corner_near(zk, i))
+                pl.when((kind == 2) & jnp.logical_not(near))(lambda i=i: self.corner_far(zk, i))
+            late = near & self.even(zk)
+            pl.when((kind == 3) & late)(lambda i=i: self.side_x(zk, i, True))
+            pl.when((kind == 3) & jnp.logical_not(late))(lambda i=i: self.side_x(zk, i, False))
         if g.L > 1:
-            send("near", self.corner_near, True)
-            send("far", self.corner_far, True)
-        send("sl", lambda zk: self.side_l(zk, False), False)
-        send("sx", lambda zk, i: self.side_x(zk, i, False), True)
-
-    def go(self, m, ahead):
-        self.step(m)
+            late = near & jnp.logical_not(self.even(zk))
+            pl.when((kind == 4) & late)(lambda: self.side_l(zk, True))
+            pl.when((kind == 4) & jnp.logical_not(late))(lambda: self.side_l(zk, False))
+        pl.when(kind == 5)(lambda: self.column(zk))
+        if extra is not None and not self.drain:
+            pl.when(kind >= 6)(lambda: extra(code - 48))
+        return jnp.where(kind == 0, jnp.where(side == 0, 1, g.X - 1), 0)
+
+    def go(self, m, ahead, work=None, extra=None, done=0):
+        count = self.step(m, work, extra, done)
 
         def wait():
             self.drain = True
@@ -736,17 +556,23 @@
             self.drain = False
 
         pl.when(m >= ahead)(wait)
-
-    def run(self, work=None, ahead=4, steps=None):
-        def one(m, carry):
-            if work is not None:
-                work(m)
-            self.go(m, ahead)
-            return carry
-
-        self.steps = steps or self.steps
-        self.ahead = ahead
-        lax.fori_loop(0, self.steps, one, 0)
+        return count
+
+    def run(self, tables, work=None, extra=None, beside=None, ahead=20):
+        self.follow(tables, ahead)
+
+        def one(m, done):
+            count = self.go(m, self.ahead, work, extra, done)
+            if beside is not None:
+                beside(m)
+            return done + count
+
+        lax.fori_loop(0, self.steps, one, jnp.int32(0))
+
+    def follow(self, tables, ahead):
+        self.tables = tables
+        self.steps = 3 * len(tables[0])
+        self.ahead = min(ahead, self.steps)
 
     def finish(self):
         self.drain = True
@@ -1094,12 +920,12 @@
 
 
 def backward_kernel(
-    layer, levels, rows, last_layer, share,
+    layer, levels, rows, last_layer,
     d_node, block, recv, npre, nnormed, nscale, rows_of, gain, ngain, node, d_before, cols_all, scale_all, d_edges, pre, normed, edges, sent,
-    w1_all, w2_all, nw1_all, nw2_all, other_grads,
-    d_node_out, d_edges_out, d_change_out, grads, tally, node_all, other_out,
+    w1_all, w2_all, nw1_all, nw2_all,
+    d_node_out, d_edges_out, d_change_out, grads, tally, node_all,
     stage, inbox, bufs, d_recv, turned, own_sum, out_buf, cols, scale, w1, w2, nw1, nw2,
-    load_sem, out_sem, send_sem, recv_sem, near_send, near_recv, *more,
+    load_sem, out_sem, send_sem, recv_sem, near_send, near_recv,
 ):
     g = Grid(levels, rows)
     h, width = d_node_out.shape
@@ -1114,12 +940,6 @@
         + ((cols_all, cols), (scale_all, scale)),
         load_sem,
     )
-    if share:
-        other_stage, other_inbox, other_total, other_send, other_recv, other_sem = more
-        other_load = pltpu.make_async_copy(other_grads, other_stage, other_sem)
-        other_load.start()
-        other = Scatter(g, other_stage, other_inbox, share, other_send, other_recv)
-        early = other.steps // 2
     rs = Scatter(g, stage, inbox, h, send_sem, recv_sem)
     wide = lambda ref: ref[layer : layer + 1, :]
     mine = pl.ds(pl.multiple_of(g.l * h, h), h)
@@ -1149,14 +969,6 @@
     grads[6 * width : 7 * width, :] = dot_tn(active, d_two).astype(BF16)
     if last_layer:
         node_all[mine, :] = node[...].astype(BF16)
-    if share:
-        other_load.wait()
-
-        def first(m, carry):
-            other.go(m, 2)
-            return carry
-
-        lax.fori_loop(0, early, first, 0)
     for copy in copies:
         copy.wait()
     copies = []
@@ -1174,8 +986,7 @@
     for copy in loads[2:]:
         copy.wait()
 
-    def work(i):
-        z, x = rs.place(i)
+    def work(z, x, i):
         pair = g.block(z, x, 0)
         start = pl.multiple_of(pair * group, 2 * group)
         place = pl.ds(start, 2 * group)
@@ -1233,25 +1044,17 @@
             stage[spot, :] = (stage[spot, :].astype(F32) + dot_nt(low, w1[2 * width :, :])).astype(BF16)
             grads[2 * width : 3 * width, :] = dot_tn(block[...], low).astype(BF16)
 
-        pl.when(i == rs.blocks - 1)(close)
-
-    def step(m):
-        pl.when(m < rs.blocks)(lambda: work(m))
-        for n, (at, left, right) in enumerate(((0, 3, 0), (1, 4, 0), (3, 1, 2))):
+        pl.when((z == g.z) & (x == g.x))(close)
+
+    def extra(n):
+        for i, (at, left, right) in enumerate(((0, 3, 0), (1, 4, 0), (3, 1, 2))):
 
             def grad(at=at, left=left, right=right):
                 grads[at * width : (at + 1) * width, :] = dot_tn(bufs[left], bufs[right]).astype(BF16)
 
-            pl.when(m == rs.blocks + n)(grad)
-        if share:
-            pl.when(m + early < other.steps)(lambda: other.go(m + early, 2))
-
-    rs.run(step)
-    if share:
-        other.ahead = 2
-        other.last(other_total)
-        other_out[...] = other_total[...].astype(BF16)
-        other.finish()
+            pl.when(n == i)(grad)
+
+    rs.run(TERMS_ORDER, work, extra)
     rs.last(turned)
     for copy in copies:
         copy.wait()
@@ -1263,7 +1066,7 @@
     rs.finish()
 
 
-def backward_layer(layer, last_layer, d_node, node_saved, cols, rows_of, scale, small, weights, d_edges, edge_saved, node, d_before, other_grads=None, share=0):
+def backward_layer(layer, last_layer, d_node, node_saved, cols, rows_of, scale, small, weights, d_edges, edge_saved, node, d_before):
     levels, rows = lax.axis_size("lvl"), lax.axis_size("row")
     width = d_node.shape[1]
     h = d_node.shape[0] // (levels if last_layer else 1)
@@ -1273,7 +1076,6 @@
     hbm = pl.BlockSpec(memory_space=pl.ANY)
     shape = jax.ShapeDtypeStruct
     ins = (d_node,) + node_saved + (rows_of,) + small + (node, d_before, cols, scale, d_edges) + edge_saved + weights
-    ins += (other_grads if share else d_before,)
     outs = (
         shape((h, width), F32),
         shape((count, width) if last_layer else (16, 128), BF16),
@@ -1281,14 +1083,13 @@
         shape((7 * width, width), BF16),
         shape((64, width), F32),
         shape((h * levels, width) if last_layer else (16, 128), BF16),
-        shape((share, width) if share else (16, 128), BF16),
     )
     others = max(levels - 1, 1)
     return pl.pallas_call(
-        functools.partial(backward_kernel, layer, levels, rows, last_layer, share),
+        functools.partial(backward_kernel, layer, levels, rows, last_layer),
         out_shape=outs,
-        in_specs=[vmem] * (len(ins) - 13) + [hbm] * 13,
-        out_specs=(vmem, hbm, hbm, vmem, vmem, vmem, vmem),
+        in_specs=[vmem] * (len(ins) - 12) + [hbm] * 12,
+        out_specs=(vmem, hbm, hbm, vmem, vmem, vmem),
         scratch_shapes=[
             pltpu.VMEM((rows * h * levels, width), BF16),
             pltpu.VMEM((Scatter.receives(levels, rows), h, width), BF16),
@@ -1308,35 +1109,23 @@
             pltpu.SemaphoreType.DMA((2 * Scatter.receives(levels, rows),)),
             pltpu.SemaphoreType.DMA((2 * others,)),
             pltpu.SemaphoreType.DMA((2 * others,)),
-                ]
-        + (
-            [
-                pltpu.VMEM((share * levels * rows, width), BF16),
-                pltpu.VMEM((Scatter.receives(levels, rows), share, width), BF16),
-                pltpu.VMEM((share, width), F32),
-                pltpu.SemaphoreType.DMA((Scatter.sends(levels, rows),)),
-                pltpu.SemaphoreType.DMA((2 * Scatter.receives(levels, rows),)),
-                pltpu.SemaphoreType.DMA,
-            ]
-            if share
-            else []
-        ),
+                ],
         compiler_params=pltpu.CompilerParams(collective_id=3 + layer, has_side_effects=True, vmem_limit_bytes=VMEM_BYTES),
         name=f"backward_{layer}",
     )(*ins)
 
 
 def sum_cuts(h):
-    return 4 if h % 64 == 0 else 1
-
-
-def sum_kernel(levels, rows, h, count, share, *refs):
-    d_node, place, update, d_change, other_piece = refs[:5]
-    terms = refs[5 : count + 5]
+    return 3 if h % 48 == 0 else 1
+
+
+def sum_kernel(levels, rows, h, count, *refs):
+    d_node, place, update, d_change = refs[:4]
+    terms = refs[4 : count + 4]
     (
-        out, d_node_all, update_out, d_change_out, other_out, stage, inbox, total,
+        out, d_node_all, update_out, d_change_out, stage, inbox, total,
         scatter_send, scatter_recv, gather_send, gather_recv, load_sem, near_send, near_recv,
-    ) = refs[count + 5 : count + 20]
+    ) = refs[count + 4 :]
     g = Grid(levels, rows)
     mine = pl.ds(pl.multiple_of(g.l * d_node.shape[0], d_node.shape[0]), d_node.shape[0])
     d_node_all[mine, :] = d_node[...].astype(BF16)
@@ -1373,44 +1162,28 @@
     rs = Scatter(g, stage, inbox, h, scatter_send, scatter_recv)
     after = tiles * 128 // size
 
-    if share:
-        other = Gather(g, other_out, share, *refs[count + 20 :])
-        other.slot(g.row, g.l)[...] = other_piece[...]
-        other.begin()
-
-    def work(m):
-        pl.when(m < after)(lambda: restore(jnp.minimum(m, after - 1)))
-        if share:
-            for s in range(2):
-                pl.when((lax.rem(m, 2) == s) & (m < 14))(lambda s=s: other.wave(m // 2, s))
-
-    rs.run(work, ahead=2, steps=max(rs.steps, 14))
+    def extra(n):
+        pl.when(n < after)(lambda: restore(jnp.minimum(n, after - 1)))
+
+    rs.run(SUM_ORDER, None, extra)
 
     def more(i, carry):
         restore(i)
         return carry
 
-    if after > rs.steps:
-        lax.fori_loop(rs.steps, after, more, 0)
+    if after > 10:
+        lax.fori_loop(10, after, more, 0)
     rs.last(total)
     ag = Courier(g, out, h, sum_cuts(h), gather_send, gather_recv)
     ag.own()[...] = total[...].astype(BF16)
-    ag.run(ORDER if ag.cuts == 4 else PLAIN_ORDER)
+    ag.run(ORDER if ag.cuts == 3 else PLAIN_ORDER)
     for copy in copies:
         copy.wait()
     rs.finish()
-    if share:
-
-        def last_waits(i, carry):
-            other.mates(i // g.X, lax.rem(i, g.X))
-            return carry
-
-        lax.fori_loop(0, 4 * g.X, last_waits, 0)
-        other.finish()
     ag.finish()
 
 
-def sum_pieces(d_node, place, update, d_change, other_piece, terms, call, share):
+def sum_pieces(d_node, place, update, d_change, terms, call):
     levels, rows = lax.axis_size("lvl"), lax.axis_size("row")
     width = terms[0].shape[1]
     count = sum(term.shape[0] for term in terms)
@@ -1418,16 +1191,15 @@
     vmem = pl.BlockSpec(memory_space=pltpu.VMEM)
     shape = jax.ShapeDtypeStruct
     return pl.pallas_call(
-        functools.partial(sum_kernel, levels, rows, h, len(terms), share),
+        functools.partial(sum_kernel, levels, rows, h, len(terms)),
         out_shape=(
             shape((count, width), BF16),
             shape((d_node.shape[0] * levels, width), BF16),
             shape(update.shape, BF16),
             shape(update.shape, BF16),
-            shape((share * levels * rows, width) if share else (16, 128), BF16),
         ),
-        in_specs=[vmem] * 5 + [pl.BlockSpec(memory_space=pl.ANY)] * len(terms),
-        out_specs=(vmem,) * 5,
+        in_specs=[vmem] * 4 + [pl.BlockSpec(memory_space=pl.ANY)] * len(terms),
+        out_specs=(vmem,) * 4,
         scratch_shapes=[
             pltpu.VMEM((count, width), BF16),
             pltpu.VMEM((Scatter.receives(levels, rows), h, width), BF16),
@@ -1439,14 +1211,13 @@
             pltpu.SemaphoreType.DMA((len(terms),)),
             pltpu.SemaphoreType.DMA((max(levels - 1, 1),)),
             pltpu.SemaphoreType.DMA((max(levels - 1, 1),)),
-        ]
-        + ([pltpu.SemaphoreType.DMA((Gather.sends(levels, rows),)), pltpu.SemaphoreType.DMA((2 * rows * levels,))] if share else []),
+        ],
         compiler_params=pltpu.CompilerParams(collective_id=call, has_side_effects=True, vmem_limit_bytes=VMEM_BYTES),
         name=f"sum_{call}",
-    )(d_node, place, update, d_change, other_piece, *terms)
-
-
-def finish_kernel(parts, smalls, update, d_change, first_sums, last_sums, node, d_node, edges, cot, edge_out, cot_out, *refs):
+    )(d_node, place, update, d_change, *terms)
+
+
+def finish_kernel(parts, smalls, update, d_change, all_sums, node, d_node, edges, cot, edge_out, cot_out, *refs):
     count = len(parts) + smalls
     wide_outs, small_outs = refs[: len(parts)], refs[len(parts) : count]
     rms_out, node_out, d_node_out, sums, rest, lows, ins, outs, wide, sums_sem, low_sem, in_sem, out_sem, wide_sem = refs[count:]
@@ -1454,8 +1225,8 @@
     steps = edges.shape[0] // size
     targets = [(n, i) for n, part in enumerate(parts) for i in range(part)]
     big = sums.shape[1]
-    loads = load_all([(ref.at[pl.ds(0, big)], sums.at[layer]) for layer, ref in enumerate((first_sums, last_sums))], sums_sem)
-    loads.append(pltpu.make_async_copy(first_sums.at[pl.ds(big, rest.shape[0])], rest, low_sem.at[4]))
+    loads = load_all([(all_sums.at[pl.ds(layer * big, big)], sums.at[layer]) for layer in range(2)], sums_sem)
+    loads.append(pltpu.make_async_copy(all_sums.at[pl.ds(2 * big, rest.shape[0])], rest, low_sem.at[4]))
     loads[-1].start()
 
     def load(step):
@@ -1514,7 +1285,7 @@
         widen(at).wait()
 
 
-def finish_all(update, d_change, first_sums, last_sums, node, d_node, edges, cot, parts, smalls):
+def finish_all(update, d_change, all_sums, node, d_node, edges, cot, parts, smalls):
     count, width = edges.shape
     size = 512 if count % 512 == 0 else 128
     vmem = pl.BlockSpec(memory_space=pltpu.VMEM)
@@ -1525,7 +1296,7 @@
     return pl.pallas_call(
         functools.partial(finish_kernel, parts, smalls),
         out_shape=wide + narrow,
-        in_specs=[hbm] * 4 + [vmem] * 2 + [hbm] * 2,
+        in_specs=[hbm] * 3 + [vmem] * 2 + [hbm] * 2,
         out_specs=(hbm,) * len(wide) + (vmem,) * len(narrow),
         scratch_shapes=[
             pltpu.VMEM((2, sum(parts) * width, width), BF16),
@@ -1542,7 +1313,7 @@
         ],
         compiler_params=pltpu.CompilerParams(vmem_limit_bytes=VMEM_BYTES),
         name="finish_all",
-    )(update, d_change, first_sums, last_sums, node, d_node, edges, cot)
+    )(update, d_change, all_sums, node, d_node, edges, cot)
 
 
 def on_device(
@@ -1570,30 +1341,25 @@
     tallies = [tally, tally_last]
     d_node = node_cotangent
     gains = (edge_gain, node_gain)
-    devices = row_total * level_total
-    even = 7 * width % (16 * devices) == 0 and devices <= 32
-    share = 7 * width // devices if even else 0
-    d_node, d_edges, d_change, last_grads, last_sums, node_all, _ = backward_layer(
+    d_node, d_edges, d_change, last_grads, last_sums, node_all = backward_layer(
         1, True, d_node, last[0], cols, rows_of, last[1], gains, weights, d_edges, last[2], node, d_edges
     )
-    if not share:
-        last_grads = lax.psum(last_grads, ("lvl", "row"))
-    d_node, _, d_change, first_grads, first_sums, _, piece = backward_layer(
-        0, False, d_node, first[0], cols, rows_of, first[1], gains, weights, d_edges, first[2], node, d_change, last_grads, share
+    d_node, _, d_change, first_grads, first_sums, _ = backward_layer(
+        0, False, d_node, first[0], cols, rows_of, first[1], gains, weights, d_edges, first[2], node, d_change
     )
     sums = [first_sums, last_sums]
     small = jnp.concatenate([jnp.sum(part.reshape(8, 8, width), axis=1) for part in sums])
     squares = jnp.stack([jnp.sum(tally.reshape(4, 8 * width), axis=1) for tally in tallies])
     squares = jnp.pad(squares.reshape(1, -1), ((0, 0), (0, width - squares.size)))
-    used = 7 * width + small.shape[0] + 1
+    devices = row_total * level_total
+    used = layers * 7 * width + small.shape[0] + 1
     each = -(-used // (16 * devices)) * 16
     rest = [small.astype(BF16), squares.astype(BF16), jnp.zeros((each * devices - used, width), BF16)]
-    flat, d_node_all, update, d_change, whole = sum_pieces(
-        d_node, place, update, d_change, piece, [first_grads, jnp.concatenate(rest)], 5, share
+    flat, d_node_all, update, d_change = sum_pieces(
+        d_node, place, update, d_change, [first_grads, last_grads, jnp.concatenate(rest)], 5
     )
-    last_grads = whole if share else last_grads
     edge_out, edge_grad, w1, w2, nw1, nw2, b1, b2, gain, shift, nb1, nb2, ngain, nshift, squares, node, d_node = finish_all(
-        update, d_change, flat, last_grads, node_all, d_node_all, edge_latent, edge_cotangent, (3, 1, 2, 1), 8
+        update, d_change, flat, node_all, d_node_all, edge_latent, edge_cotangent, (3, 1, 2, 1), 8
     )
     node_entries = float(node_count * row_total * width)
     edge_entries = float(edge_count * row_total * level_total * width)

time: 391 us -> 371 us (0.949)
  the two profiles are of different devices: /device:TPU:0 before, /device:TPU:1 now
where the time goes in v1:
time: 371 us; the launch traced here: 364 us
  Pallas kernels  357 us (96%)
  other arithmetic  3.81 us (1%)
    pallas_call x2, Pallas kernels, backward_layer(): pl.pallas_call(functools.partial(backward_kernel, layer, levels, rows, la...  129 us
    pallas_call x2, Pallas kernels, forward_layer(): pl.pallas_call(functools.partial(forward_kernel, layer, levels, rows, fir...  120 us
    pallas_call x1, Pallas kernels, sum_pieces(): pl.pallas_call(functools.partial(sum_kernel, levels, rows, h, len(terms))...  89.5 us
    pallas_call x1, Pallas kernels, finish_all(): pl.pallas_call(functools.partial(finish_kernel, parts, smalls), out_shape...  19.2 us

profile of v1, /device:TPU:1, one launch (start us, length us, event | category | flops | bytes accessed | tf_op | source)
XLA Modules:
  0.0 363.7 jit_solution(14602973594127584902)
XLA Ops:
  1.3 0.1 pad.9.clone
  1.4 62.2 %forward_0.1 = (bf16[2560,512]{1,0:T(8,128)(2,1)}, bf16[2560,512]{1,0:T(8,128)(2,1)}, bf16[2560,512]{1,0:T(8,128)(2,1)}, bf16[2560,512]{1,0:T(8,128)(2,1)}, bf16...) custom-call(f32[512,512]{1,0:T(8,128)} %refs_0_.1, ...), custom_call_target="tpu_custom_call" | custom-call | tf_op jit(solution)/shard_map/forward_0/pallas_call | solution.py:889
  63.6 1.0 reduce_sum.52
  64.5 0.1 reduce_sum.53
  64.6 0.1 reduce_sum.54
  64.7 57.3 %forward_1.1 = (bf16[2560,512]{1,0:T(8,128)(2,1)}, bf16[2560,512]{1,0:T(8,128)(2,1)}, bf16[2560,512]{1,0:T(8,128)(2,1)}, bf16[2560,512]{1,0:T(8,128)(2,1)}, bf16...) custom-call(f32[256,512]{1,0:T(8,128)} %get-tuple-element.78.refs_0_, ...), custom_call_target="tpu_custom_call" | custom-call | tf_op jit(solution)/shard_map/forward_1/pallas_call | solution.py:889
  122.1 64.1 %backward_1.1 = (f32[256,512]{1,0:T(8,128)}, bf16[2560,512]{1,0:T(8,128)(2,1)}, bf16[2560,512]{1,0:T(8,128)(2,1)}, bf16[3584,512]{1,0:T(8,128)(2,1)}, f32[64,512]{1,0:T(8,128)}, /*index=5*/bf16[512,512]{1,0:T(8,128)(2,1)}) custom-call(f32[512,512]{1,0:T(8,128)} %d_node.1, bf16[512,512]{1,0:T(8,128)(2,1)} %get-tuple-element.84.block, ...), custom_call_target="tpu_custom_call" | custom-call | tf_op jit(solution)/shard_map/backward_1/pallas_call | solution.py:1088
  186.2 0.0 copy-start
  186.2 0.0 copy-start.1
  186.2 64.9 %backward_0.1 = (f32[256,512]{1,0:T(8,128)}, bf16[16,128]{1,0:T(8,128)(2,1)}, bf16[2560,512]{1,0:T(8,128)(2,1)}, bf16[3584,512]{1,0:T(8,128)(2,1)}, f32[64,512]{1,0:T(8,128)}, /*index=5*/bf16[16,128]{1,0:T(8,128)(2,1)}) custom-call(f32[256,512]{1,0:T(8,128)} %get-tuple-element.95.d_node, bf16[512,512]{1,0:T(8,128)(2,1)} %get-tuple-element.96.block, ...), custom_call_target="tpu_custom_call" | custom-call | tf_op jit(solution)/shard_map/backward_0/pallas_call | solution.py:1088
  251.1 0.0 copy-done
  251.1 1.0 bitcast_reduce_fusion
  252.1 0.0 copy-done.1
  252.1 0.1 reduce_sum.55
  252.2 0.1 reduce_sum.56
  252.3 0.1 reduce_sum.57
  252.5 0.1 reshape.63
  252.5 0.9 fusion.3.refs_6_
  253.5 89.5 %sum_5.1 = (bf16[7680,512]{1,0:T(8,128)(2,1)}, bf16[512,512]{1,0:T(8,128)(2,1)}, bf16[2560,512]{1,0:T(8,128)(2,1)}, bf16[2560,512]{1,0:T(8,128)(2,1)}) custom-call(f32[256,512]{1,0:T(8,128)} %get-tuple-element.108.refs_0_, s32[20,128]{1,0:T(8,128)} %get-tuple-element.79.refs_14_.refs_1_, bf16[2560,512]{1,0:T(8,128)(2,1)} %get-tuple-element.109.refs_2_, ...), custom_call_target="tpu_custom_call" | custom-call | tf_op jit(solution)/shard_map/sum_5/pallas_call | solution.py:1193
  342.9 0.0 copy-start.2
  342.9 19.2 %finish_all.1 = (f32[2560,512]{1,0:T(8,128)}, f32[2560,512]{1,0:T(8,128)}, f32[2,1536,512]{2,1,0:T(8,128)}, f32[2,512,512]{2,1,0:T(8,128)}, f32[2,1024,512]{2,1,...) custom-call(bf16[2560,512]{1,0:T(8,128)(2,1)} %get-tuple-element.117, ...), custom_call_target="tpu_custom_call" | custom-call | tf_op jit(solution)/shard_map/finish_all/pallas_call | solution.py:1296
  362.2 0.6 slice_reduce_fusion
  362.8 0.1 reshape_squeeze.3
  362.9 0.0 copy-done.2
  362.9 0.6 multiply_sqrt_fusion
  (2 shorter events, 0.0 us)
Async XLA Ops:
  186.2 64.9 %copy-start = (f32[64,512]{1,0:T(8,128)S(1)}, f32[64,512]{1,0:T(8,128)}, u32[]{:S(2)}) copy-start(f32[64,512]{1,0:T(8,128)} %get-tuple-element.114) | copy-start | bytes 393220
  186.2 65.9 %copy-start.1 = (f32[32,512]{1,0:T(8,128)S(1)}, f32[32,512]{1,0:T(8,128)}, u32[]{:S(2)}) copy-start(f32[32,512]{1,0:T(8,128)} %get-tuple-element.116) | copy-start | bytes 196612
  342.9 20.0 %copy-start.2 = (f32[4]{0:T(128)S(1)}, f32[4]{0:T(128)}, u32[]{:S(2)}) copy-start(f32[4]{0:T(128)} %constant.13) | copy-start | bytes 52

commit v2 on v1

--- a/solution.py
+++ b/solution.py
@@ -14,7 +14,7 @@
 VMEM_BYTES = 61 * 2**20
 
 
-WORK_ORDER = (
+FIRST_ORDER = (
     (
         1089728, 289296, 536069, 551556, 141360, 612561, 159764, 1528408, 356492, 400397,
         858841, 422440, 750249, 990892, 1707549, 1799737, 2097129,
@@ -24,22 +24,32 @@
         290876, 745128, 724581, 482457, 1774801, 1717985, 2097129,
     ),
 )
+LAST_ORDER = (
+    (
+        1089728, 526421, 84180, 1507921, 141360, 1530017, 159781, 1462872, 880781, 919081,
+        330920, 854680, 745060, 480869, 466664, 1799737, 2097129,
+    ),
+    (
+        1089728, 600797, 338944, 607233, 154201, 214620, 1378337, 920240, 815648, 988240,
+        1575989, 1004689, 415277, 937573, 487633, 1734248, 2097133,
+    ),
+)
 ORDER = (
     (
-        280580, 295586, 590612, 803888, 167948, 151730, 217752, 235036, 693301, 365337,
-        855736, 760990, 986429, 740022, 679230,
+        67728, 295584, 137222, 165041, 594213, 203041, 216120, 630414, 724277, 691860,
+        860188, 365736, 744729, 986937, 1022741, 2097070,
     ),
     (
-        589832, 607380, 32934, 214538, 233524, 808981, 412469, 678712, 548394, 269996,
-        657586, 741656, 1023289, 464658, 479002,
+        133632, 152228, 17702, 199298, 856077, 808974, 678584, 985110, 727841, 416061,
+        942120, 693914, 563002, 286492, 397085, 2097042,
     ),
 )
 PLAIN_ORDER = (
     (
-        524816, 133680, 394788, 465448, 990252,
+        524816, 133680, 204836, 857112, 923164, 2097084,
     ),
     (
-        328704, 526372, 658444, 464948, 990252,
+        328704, 526372, 401420, 793128, 923164, 2097084,
     ),
 )
 
@@ -55,12 +65,12 @@
 )
 SUM_ORDER = (
     (
-        82311, 251910, 65686, 820894, 329484, 902566, 809372, 917796, 300826, 1162,
-        562704, 525336, 890169, 2087477,
+        66311, 934531, 232207, 21296, 36621, 331276, 591287, 835634, 760841, 267794,
+        804122, 399906, 888840, 2087594,
     ),
     (
-        792839, 83844, 884894, 803212, 212998, 591254, 296090, 40115, 329752, 135950,
-        525623, 871970, 661038, 2087480,
+        786951, 246531, 82078, 181810, 367396, 3346, 214199, 329752, 230402, 529162,
+        466099, 563374, 922668, 2087604,
     ),
 )
 
@@ -813,7 +823,7 @@
         for copy in leave(n, part):
             copy.start()
 
-    ag.run(WORK_ORDER, meanwhile, prepare, work)
+    ag.run(FIRST_ORDER if first_layer else LAST_ORDER, meanwhile, prepare, work)
     copies = []
     for j in range(1, levels):
         l, l_dev = g.l_other(j)
@@ -1120,12 +1130,12 @@
 
 
 def sum_kernel(levels, rows, h, count, *refs):
-    d_node, place, update, d_change = refs[:4]
-    terms = refs[4 : count + 4]
+    d_node, place, sums, last_sums, tally, last_tally, update_all, d_change_all = refs[:8]
+    terms = refs[8 : count + 8]
     (
-        out, d_node_all, update_out, d_change_out, stage, inbox, total,
-        scatter_send, scatter_recv, gather_send, gather_recv, load_sem, near_send, near_recv,
-    ) = refs[count + 4 :]
+        out, d_node_all, update_out, d_change_out, stage, inbox, total, update, d_change, back,
+        scatter_send, scatter_recv, gather_send, gather_recv, load_sem, back_sem, near_send, near_recv,
+    ) = refs[count + 8 :]
     g = Grid(levels, rows)
     mine = pl.ds(pl.multiple_of(g.l * d_node.shape[0], d_node.shape[0]), d_node.shape[0])
     d_node_all[mine, :] = d_node[...].astype(BF16)
@@ -1134,20 +1144,42 @@
     for term in terms:
         pairs.append((term, stage.at[pl.ds(at, term.shape[0])]))
         at += term.shape[0]
+    pairs += [(update_all, update), (d_change_all, d_change)]
     loads = load_all(pairs, load_sem)
+    width = stage.shape[1]
+    lanes = lax.broadcasted_iota(jnp.int32, (16, width), 1)
+    subs = lax.broadcasted_iota(jnp.int32, (16, width), 0)
+    squares = jnp.zeros((16, width), F32)
+    for layer, ref in enumerate((tally, last_tally)):
+        for i in range(4):
+            part = jnp.sum(jnp.sum(ref[8 * i : 8 * i + 8, :], axis=0, keepdims=True), axis=1, keepdims=True)
+            squares = jnp.where((subs == 0) & (lanes == 4 * layer + i), part, squares)
+    few = [jnp.sum(ref[...].reshape(8, 8, width), axis=1) for ref in (sums, last_sums)]
+    stage[at : at + 16, :] = jnp.concatenate(few, axis=0).astype(BF16)
+    stage[at + 16 : at + 32, :] = squares.astype(BF16)
+    if stage.shape[0] > at + 32:
+        stage[at + 32 :, :] = jnp.zeros((stage.shape[0] - at - 32, width), BF16)
     g.greet()
     for copy in loads:
         copy.wait()
-    copies = []
-    for j in range(1, levels):
-        copy = pltpu.make_async_remote_copy(
+    copies = [
+        pltpu.make_async_remote_copy(
             d_node_all.at[mine], d_node_all.at[mine], near_send.at[j - 1], near_recv.at[levels - 1 - j], device_id=g.l_other(j)[1], device_id_type=MESH
         )
-        copy.start()
-        copies.append(copy)
+        for j in range(1, levels)
+    ]
+
+    def exchange(at):
+        for copy in copies if at == 0 else ():
+            copy.start()
+
     tiles = place.shape[0]
     size = 256 if tiles % 2 == 0 else 128
     lane = lax.broadcasted_iota(jnp.int32, (128, 128), 1).astype(F32)
+
+    def leave(i):
+        here = pl.ds(pl.multiple_of(i * size, size), size)
+        return [pltpu.make_async_copy(back.at[i, n], ref.at[here], back_sem.at[i, n]) for n, ref in enumerate((update_out, d_change_out))]
 
     def restore(i):
         pick = []
@@ -1155,9 +1187,10 @@
             spot = jnp.broadcast_to(place[pl.ds(i * (size // 128) + part, 1), :], (128, 128)).astype(F32).T
             pick.append(jnp.concatenate([(spot == lane + float(128 * j)).astype(BF16) for j in range(tiles)], axis=1))
         pick = jnp.concatenate(pick, axis=0)
-        here = pl.ds(pl.multiple_of(i * size, size), size)
-        update_out[here, :] = dot(pick, update[...]).astype(BF16)
-        d_change_out[here, :] = dot(pick, d_change[...]).astype(BF16)
+        back[i, 0] = dot(pick, update[...]).astype(BF16)
+        back[i, 1] = dot(pick, d_change[...]).astype(BF16)
+        for copy in leave(i):
+            copy.start()
 
     rs = Scatter(g, stage, inbox, h, scatter_send, scatter_recv)
     after = tiles * 128 // size
@@ -1176,20 +1209,27 @@
     rs.last(total)
     ag = Courier(g, out, h, sum_cuts(h), gather_send, gather_recv)
     ag.own()[...] = total[...].astype(BF16)
-    ag.run(ORDER if ag.cuts == 3 else PLAIN_ORDER)
+    ag.run(ORDER if ag.cuts == 3 else PLAIN_ORDER, exchange)
     for copy in copies:
         copy.wait()
+    for i in range(after):
+        for copy in leave(i):
+            copy.wait()
     rs.finish()
     ag.finish()
 
 
-def sum_pieces(d_node, place, update, d_change, terms, call):
+def sum_pieces(d_node, place, small, update, d_change, terms, call):
     levels, rows = lax.axis_size("lvl"), lax.axis_size("row")
     width = terms[0].shape[1]
-    count = sum(term.shape[0] for term in terms)
-    h = count // (levels * rows)
+    used = sum(term.shape[0] for term in terms) + 32
+    h = -(-used // (16 * levels * rows)) * 16
+    count = h * levels * rows
     vmem = pl.BlockSpec(memory_space=pltpu.VMEM)
+    hbm = pl.BlockSpec(memory_space=pl.ANY)
     shape = jax.ShapeDtypeStruct
+    tiles = update.shape[0] // 128
+    size = 256 if tiles % 2 == 0 else 128
     return pl.pallas_call(
         functools.partial(sum_kernel, levels, rows, h, len(terms)),
         out_shape=(
@@ -1198,77 +1238,74 @@
             shape(update.shape, BF16),
             shape(update.shape, BF16),
         ),
-        in_specs=[vmem] * 4 + [pl.BlockSpec(memory_space=pl.ANY)] * len(terms),
-        out_specs=(vmem,) * 4,
+        in_specs=[vmem] * 6 + [hbm] * (2 + len(terms)),
+        out_specs=(vmem, vmem, hbm, hbm),
         scratch_shapes=[
             pltpu.VMEM((count, width), BF16),
             pltpu.VMEM((Scatter.receives(levels, rows), h, width), BF16),
             pltpu.VMEM((h, width), F32),
+            pltpu.VMEM(update.shape, BF16),
+            pltpu.VMEM(update.shape, BF16),
+            pltpu.VMEM((tiles * 128 // size, 2, size, width), BF16),
             pltpu.SemaphoreType.DMA((Scatter.sends(levels, rows),)),
             pltpu.SemaphoreType.DMA((2 * Scatter.receives(levels, rows),)),
             pltpu.SemaphoreType.DMA((Courier.sends(levels, rows, sum_cuts(h)),)),
             pltpu.SemaphoreType.DMA((Courier.receives(levels, rows, sum_cuts(h)),)),
-            pltpu.SemaphoreType.DMA((len(terms),)),
+            pltpu.SemaphoreType.DMA((len(terms) + 2,)),
+            pltpu.SemaphoreType.DMA((tiles * 128 // size, 2)),
             pltpu.SemaphoreType.DMA((max(levels - 1, 1),)),
             pltpu.SemaphoreType.DMA((max(levels - 1, 1),)),
         ],
         compiler_params=pltpu.CompilerParams(collective_id=call, has_side_effects=True, vmem_limit_bytes=VMEM_BYTES),
         name=f"sum_{call}",
-    )(d_node, place, update, d_change, *terms)
+    )(d_node, place, *small, update, d_change, *terms)
 
 
 def finish_kernel(parts, smalls, update, d_change, all_sums, node, d_node, edges, cot, edge_out, cot_out, *refs):
     count = len(parts) + smalls
     wide_outs, small_outs = refs[: len(parts)], refs[len(parts) : count]
-    rms_out, node_out, d_node_out, sums, rest, lows, ins, outs, wide, sums_sem, low_sem, in_sem, out_sem, wide_sem = refs[count:]
+    rms_out, node_out, d_node_out, sums, rest, lows, ins, outs, wide, sums_sem, rest_sem, low_sem, in_sem, out_sem, wide_sem = refs[count:]
     size, width = ins.shape[2:]
     steps = edges.shape[0] // size
     targets = [(n, i) for n, part in enumerate(parts) for i in range(part)]
     big = sums.shape[1]
     loads = load_all([(all_sums.at[pl.ds(layer * big, big)], sums.at[layer]) for layer in range(2)], sums_sem)
-    loads.append(pltpu.make_async_copy(all_sums.at[pl.ds(2 * big, rest.shape[0])], rest, low_sem.at[4]))
+    loads.append(pltpu.make_async_copy(all_sums.at[pl.ds(2 * big, rest.shape[0])], rest, rest_sem))
     loads[-1].start()
 
     def load(step):
         here = pl.ds(step * size, size)
-        pairs = ((edges, ins.at[step % 2, 0], in_sem.at[step % 2, 0]), (cot, ins.at[step % 2, 1], in_sem.at[step % 2, 1]))
-        pairs += ((update, lows.at[step % 2, 0], low_sem.at[step % 2 * 2]), (d_change, lows.at[step % 2, 1], low_sem.at[step % 2 * 2 + 1]))
+        pairs = ((edges, ins.at[step, 0], in_sem.at[step, 0]), (cot, ins.at[step, 1], in_sem.at[step, 1]))
+        pairs += ((update, lows.at[step, 0], low_sem.at[step, 0]), (d_change, lows.at[step, 1], low_sem.at[step, 1]))
         return [pltpu.make_async_copy(ref.at[here], to, sem) for ref, to, sem in pairs]
 
     def leave(step):
         here = pl.ds(step * size, size)
-        return [pltpu.make_async_copy(outs.at[step % 2, n], ref.at[here], out_sem.at[step % 2, n]) for n, ref in enumerate((edge_out, cot_out))]
+        return [pltpu.make_async_copy(outs.at[step, n], ref.at[here], out_sem.at[step, n]) for n, ref in enumerate((edge_out, cot_out))]
 
     def widen(at):
         n, i = targets[at % len(targets)]
         ref = wide_outs[n].at[at // len(targets), pl.ds(i * width, width)]
-        return pltpu.make_async_copy(wide.at[at % 4], ref, wide_sem.at[at % 4])
+        return pltpu.make_async_copy(wide.at[at], ref, wide_sem.at[at])
 
     total = 2 * len(targets)
     done = 0
-    for copy in load(0):
-        copy.start()
     for step in range(steps):
-        if step + 1 < steps:
-            for copy in load(step + 1):
-                copy.start()
+        for copy in load(step):
+            copy.start()
+    for step in range(steps):
         for copy in load(step):
             copy.wait()
-        if step >= 2:
-            for copy in leave(step - 2):
-                copy.wait()
         for n in range(2):
-            outs[step % 2, n] = ins[step % 2, n] + lows[step % 2, n].astype(F32)
+            outs[step, n] = ins[step, n] + lows[step, n].astype(F32)
         for copy in leave(step):
             copy.start()
         if step == 0:
             for copy in loads:
                 copy.wait()
         while done < total * (step + 1) // steps:
-            if done >= 4:
-                widen(done - 4).wait()
             layer, at = done // len(targets), done % len(targets)
-            wide[done % 4] = sums[layer, at * width : (at + 1) * width, :].astype(F32)
+            wide[done] = sums[layer, at * width : (at + 1) * width, :].astype(F32)
             widen(done).start()
             done += 1
     few = rest[...].astype(F32)
@@ -1278,10 +1315,10 @@
     rms_out[...] = few[2 * smalls : 2 * smalls + 1]
     node_out[...] = node[...].astype(F32)
     d_node_out[...] = d_node[...].astype(F32)
-    for step in range(max(steps - 2, 0), steps):
+    for step in range(steps):
         for copy in leave(step):
             copy.wait()
-    for at in range(total - 4, total):
+    for at in range(total):
         widen(at).wait()
 
 
@@ -1301,15 +1338,16 @@
         scratch_shapes=[
             pltpu.VMEM((2, sum(parts) * width, width), BF16),
             pltpu.VMEM((32, width), BF16),
-            pltpu.VMEM((2, 2, size, width), BF16),
-            pltpu.VMEM((2, 2, size, width), F32),
-            pltpu.VMEM((2, 2, size, width), F32),
-            pltpu.VMEM((4, width, width), F32),
+            pltpu.VMEM((count // size, 2, size, width), BF16),
+            pltpu.VMEM((count // size, 2, size, width), F32),
+            pltpu.VMEM((count // size, 2, size, width), F32),
+            pltpu.VMEM((2 * sum(parts), width, width), F32),
             pltpu.SemaphoreType.DMA((2,)),
-            pltpu.SemaphoreType.DMA((5,)),
-            pltpu.SemaphoreType.DMA((2, 2)),
-            pltpu.SemaphoreType.DMA((2, 2)),
-            pltpu.SemaphoreType.DMA((4,)),
+            pltpu.SemaphoreType.DMA,
+            pltpu.SemaphoreType.DMA((count // size, 2)),
+            pltpu.SemaphoreType.DMA((count // size, 2)),
+            pltpu.SemaphoreType.DMA((count // size, 2)),
+            pltpu.SemaphoreType.DMA((2 * sum(parts),)),
         ],
         compiler_params=pltpu.CompilerParams(vmem_limit_bytes=VMEM_BYTES),
         name="finish_all",
@@ -1338,7 +1376,6 @@
         1, node, small, weights, edge_cotangent, (place, rows_of, cols), edges_next, update
     )
     last = ((block, recv, npre, nnormed, nscale), scale, (pre, normed, edges_next, sent))
-    tallies = [tally, tally_last]
     d_node = node_cotangent
     gains = (edge_gain, node_gain)
     d_node, d_edges, d_change, last_grads, last_sums, node_all = backward_layer(
@@ -1347,16 +1384,8 @@
     d_node, _, d_change, first_grads, first_sums, _ = backward_layer(
         0, False, d_node, first[0], cols, rows_of, first[1], gains, weights, d_edges, first[2], node, d_change
     )
-    sums = [first_sums, last_sums]
-    small = jnp.concatenate([jnp.sum(part.reshape(8, 8, width), axis=1) for part in sums])
-    squares = jnp.stack([jnp.sum(tally.reshape(4, 8 * width), axis=1) for tally in tallies])
-    squares = jnp.pad(squares.reshape(1, -1), ((0, 0), (0, width - squares.size)))
-    devices = row_total * level_total
-    used = layers * 7 * width + small.shape[0] + 1
-    each = -(-used // (16 * devices)) * 16
-    rest = [small.astype(BF16), squares.astype(BF16), jnp.zeros((each * devices - used, width), BF16)]
     flat, d_node_all, update, d_change = sum_pieces(
-        d_node, place, update, d_change, [first_grads, last_grads, jnp.concatenate(rest)], 5
+        d_node, place, (first_sums, last_sums, tally, tally_last), update, d_change, [first_grads, last_grads], 5
     )
     edge_out, edge_grad, w1, w2, nw1, nw2, b1, b2, gain, shift, nb1, nb2, ngain, nshift, squares, node, d_node = finish_all(
         update, d_change, flat, node_all, d_node_all, edge_latent, edge_cotangent, (3, 1, 2, 1), 8

time: 371 us -> 364 us (0.981)
  the two profiles are of different devices: /device:TPU:1 before, /device:TPU:0 now
where the time goes in v2:
time: 364 us; the launch traced here: 357 us
  Pallas kernels  354 us (97%)
    pallas_call x2, Pallas kernels, backward_layer(): pl.pallas_call(functools.partial(backward_kernel, layer, levels, rows, la...  126 us
    pallas_call x2, Pallas kernels, forward_layer(): pl.pallas_call(functools.partial(forward_kernel, layer, levels, rows, fir...  122 us
    pallas_call x1, Pallas kernels, sum_pieces(): pl.pallas_call(functools.partial(sum_kernel, levels, rows, h, len(terms))...  87 us
    pallas_call x1, Pallas kernels, finish_all(): pl.pallas_call(functools.partial(finish_kernel, parts, smalls), out_shape...  18.7 us

profile of v2, /device:TPU:0, one launch (start us, length us, event | category | flops | bytes accessed | tf_op | source)
XLA Modules:
  0.0 356.8 jit_solution(1589352063089000725)
XLA Ops:
  1.3 65.1 %forward_0.1 = (bf16[2560,512]{1,0:T(8,128)(2,1)}, bf16[2560,512]{1,0:T(8,128)(2,1)}, bf16[2560,512]{1,0:T(8,128)(2,1)}, bf16[2560,512]{1,0:T(8,128)(2,1)}, bf16...) custom-call(f32[512,512]{1,0:T(8,128)} %refs_0_.1, ...), custom_call_target="tpu_custom_call" | custom-call | tf_op jit(solution)/shard_map/forward_0/pallas_call | solution.py:899
  66.4 57.0 %forward_1.1 = (bf16[2560,512]{1,0:T(8,128)(2,1)}, bf16[2560,512]{1,0:T(8,128)(2,1)}, bf16[2560,512]{1,0:T(8,128)(2,1)}, bf16[2560,512]{1,0:T(8,128)(2,1)}, bf16...) custom-call(f32[256,512]{1,0:T(8,128)} %get-tuple-element.78.refs_0_, ...), custom_call_target="tpu_custom_call" | custom-call | tf_op jit(solution)/shard_map/forward_1/pallas_call | solution.py:899
  123.4 61.5 %backward_1.1 = (f32[256,512]{1,0:T(8,128)}, bf16[2560,512]{1,0:T(8,128)(2,1)}, bf16[2560,512]{1,0:T(8,128)(2,1)}, bf16[3584,512]{1,0:T(8,128)(2,1)}, f32[64,512]{1,0:T(8,128)}, /*index=5*/bf16[512,512]{1,0:T(8,128)(2,1)}) custom-call(f32[512,512]{1,0:T(8,128)} %d_node.1, bf16[512,512]{1,0:T(8,128)(2,1)} %get-tuple-element.84.block, ...), custom_call_target="tpu_custom_call" | custom-call | tf_op jit(solution)/shard_map/backward_1/pallas_call | solution.py:1098
  184.9 64.6 %backward_0.1 = (f32[256,512]{1,0:T(8,128)}, bf16[16,128]{1,0:T(8,128)(2,1)}, bf16[2560,512]{1,0:T(8,128)(2,1)}, bf16[3584,512]{1,0:T(8,128)(2,1)}, f32[64,512]{1,0:T(8,128)}, /*index=5*/bf16[16,128]{1,0:T(8,128)(2,1)}) custom-call(f32[256,512]{1,0:T(8,128)} %get-tuple-element.95.d_node, bf16[512,512]{1,0:T(8,128)(2,1)} %get-tuple-element.96.block, ...), custom_call_target="tpu_custom_call" | custom-call | tf_op jit(solution)/shard_map/backward_0/pallas_call | solution.py:1098
  249.5 87.0 %sum_5.1 = (bf16[7680,512]{1,0:T(8,128)(2,1)}, bf16[512,512]{1,0:T(8,128)(2,1)}, bf16[2560,512]{1,0:T(8,128)(2,1)}, bf16[2560,512]{1,0:T(8,128)(2,1)}) custom-call(f32[256,512]{1,0:T(8,128)} %get-tuple-element.108.refs_0_, s32[20,128]{1,0:T(8,128)} %get-tuple-element.79.refs_14_.refs_1_, f32[64,512]{1,0:T(8,128)} %get-tuple-element.109.refs_2_, ...), custom_call_target="tpu_custom_call" | custom-call | tf_op jit(solution)/shard_map/sum_5/pallas_call | solution.py:1233
  336.6 0.0 copy-start
  336.6 18.7 %finish_all.1 = (f32[2560,512]{1,0:T(8,128)}, f32[2560,512]{1,0:T(8,128)}, f32[2,1536,512]{2,1,0:T(8,128)}, f32[2,512,512]{2,1,0:T(8,128)}, f32[2,1024,512]{2,1,...) custom-call(bf16[2560,512]{1,0:T(8,128)(2,1)} %get-tuple-element.117, ...), custom_call_target="tpu_custom_call" | custom-call | tf_op jit(solution)/shard_map/finish_all/pallas_call | solution.py:1333
  355.3 0.6 slice_reduce_fusion
  356.0 0.1 reshape_squeeze.3
  356.0 0.0 copy-done
  356.0 0.6 multiply_sqrt_fusion
Async XLA Ops:
  336.6 19.5 %copy-start = (f32[4]{0:T(128)S(1)}, f32[4]{0:T(128)}, u32[]{:S(2)}) copy-start(f32[4]{0:T(128)} %constant.4) | copy-start | bytes 52

commit v3 on v2

--- a/solution.py
+++ b/solution.py
@@ -55,22 +55,22 @@
 
 TERMS_ORDER = (
     (
-        246535, 230038, 329348, 54046, 34332, 180388, 147502, 722962, 432138, 820258,
-        692248, 2097073,
+        246535, 84766, 213518, 51750, 36364, 21003, 153362, 722970, 4362, 527368,
+        809258, 2097072,
     ),
     (
-        115332, 247427, 184844, 19218, 328838, 233232, 463616, 397320, 431874, 558380,
-        825512, 2097072,
+        115201, 197251, 362404, 149771, 493190, 2068, 463630, 33816, 431904, 563210,
+        807980, 2097074,
     ),
 )
 SUM_ORDER = (
     (
-        66311, 934531, 232207, 21296, 36621, 331276, 591287, 835634, 760841, 267794,
-        804122, 399906, 888840, 2087594,
+        934663, 362370, 491653, 623118, 213428, 149012, 460196, 169728, 793232, 428296,
+        891820, 921634, 808216, 2087219,
     ),
     (
-        786951, 246531, 82078, 181810, 367396, 3346, 214199, 329752, 230402, 529162,
-        466099, 563374, 922668, 2087604,
+        787329, 50308, 100229, 196638, 823824, 187277, 232210, 330808, 131382, 466086,
+        167200, 562997, 807980, 2087475,
     ),
 )
 

time: 364 us -> 358 us (0.984)
  Pallas kernels: 354 us -> 348 us
where the time goes in v3:
time: 358 us; the launch traced here: 351 us
  Pallas kernels  348 us (97%)
    pallas_call x2, Pallas kernels, backward_layer(): pl.pallas_call(functools.partial(backward_kernel, layer, levels, rows, la...  123 us
    pallas_call x2, Pallas kernels, forward_layer(): pl.pallas_call(functools.partial(forward_kernel, layer, levels, rows, fir...  122 us
    pallas_call x1, Pallas kernels, sum_pieces(): pl.pallas_call(functools.partial(sum_kernel, levels, rows, h, len(terms))...  83.8 us
    pallas_call x1, Pallas kernels, finish_all(): pl.pallas_call(functools.partial(finish_kernel, parts, smalls), out_shape...  18.7 us

profile of v3, /device:TPU:0, one launch (start us, length us, event | category | flops | bytes accessed | tf_op | source)
XLA Modules:
  0.0 351.0 jit_solution(2140805549831361476)
XLA Ops:
  1.3 65.1 %forward_0.1 = (bf16[2560,512]{1,0:T(8,128)(2,1)}, bf16[2560,512]{1,0:T(8,128)(2,1)}, bf16[2560,512]{1,0:T(8,128)(2,1)}, bf16[2560,512]{1,0:T(8,128)(2,1)}, bf16...) custom-call(f32[512,512]{1,0:T(8,128)} %refs_0_.1, ...), custom_call_target="tpu_custom_call" | custom-call | tf_op jit(solution)/shard_map/forward_0/pallas_call | solution.py:899
  66.4 57.0 %forward_1.1 = (bf16[2560,512]{1,0:T(8,128)(2,1)}, bf16[2560,512]{1,0:T(8,128)(2,1)}, bf16[2560,512]{1,0:T(8,128)(2,1)}, bf16[2560,512]{1,0:T(8,128)(2,1)}, bf16...) custom-call(f32[256,512]{1,0:T(8,128)} %get-tuple-element.78.refs_0_, ...), custom_call_target="tpu_custom_call" | custom-call | tf_op jit(solution)/shard_map/forward_1/pallas_call | solution.py:899
  123.4 60.3 %backward_1.1 = (f32[256,512]{1,0:T(8,128)}, bf16[2560,512]{1,0:T(8,128)(2,1)}, bf16[2560,512]{1,0:T(8,128)(2,1)}, bf16[3584,512]{1,0:T(8,128)(2,1)}, f32[64,512]{1,0:T(8,128)}, /*index=5*/bf16[512,512]{1,0:T(8,128)(2,1)}) custom-call(f32[512,512]{1,0:T(8,128)} %d_node.1, bf16[512,512]{1,0:T(8,128)(2,1)} %get-tuple-element.84.block, ...), custom_call_target="tpu_custom_call" | custom-call | tf_op jit(solution)/shard_map/backward_1/pallas_call | solution.py:1098
  183.8 63.1 %backward_0.1 = (f32[256,512]{1,0:T(8,128)}, bf16[16,128]{1,0:T(8,128)(2,1)}, bf16[2560,512]{1,0:T(8,128)(2,1)}, bf16[3584,512]{1,0:T(8,128)(2,1)}, f32[64,512]{1,0:T(8,128)}, /*index=5*/bf16[16,128]{1,0:T(8,128)(2,1)}) custom-call(f32[256,512]{1,0:T(8,128)} %get-tuple-element.95.d_node, bf16[512,512]{1,0:T(8,128)(2,1)} %get-tuple-element.96.block, ...), custom_call_target="tpu_custom_call" | custom-call | tf_op jit(solution)/shard_map/backward_0/pallas_call | solution.py:1098
  246.9 83.8 %sum_5.1 = (bf16[7680,512]{1,0:T(8,128)(2,1)}, bf16[512,512]{1,0:T(8,128)(2,1)}, bf16[2560,512]{1,0:T(8,128)(2,1)}, bf16[2560,512]{1,0:T(8,128)(2,1)}) custom-call(f32[256,512]{1,0:T(8,128)} %get-tuple-element.108.refs_0_, s32[20,128]{1,0:T(8,128)} %get-tuple-element.79.refs_14_.refs_1_, f32[64,512]{1,0:T(8,128)} %get-tuple-element.109.refs_2_, ...), custom_call_target="tpu_custom_call" | custom-call | tf_op jit(solution)/shard_map/sum_5/pallas_call | solution.py:1233
  330.8 0.0 copy-start
  330.8 18.7 %finish_all.1 = (f32[2560,512]{1,0:T(8,128)}, f32[2560,512]{1,0:T(8,128)}, f32[2,1536,512]{2,1,0:T(8,128)}, f32[2,512,512]{2,1,0:T(8,128)}, f32[2,1024,512]{2,1,...) custom-call(bf16[2560,512]{1,0:T(8,128)(2,1)} %get-tuple-element.117, ...), custom_call_target="tpu_custom_call" | custom-call | tf_op jit(solution)/shard_map/finish_all/pallas_call | solution.py:1333
  349.5 0.6 slice_reduce_fusion
  350.2 0.1 reshape_squeeze.3
  350.2 0.0 copy-done
  350.2 0.6 multiply_sqrt_fusion
Async XLA Ops:
  330.8 19.5 %copy-start = (f32[4]{0:T(128)S(1)}, f32[4]{0:T(128)}, u32[]{:S(2)}) copy-start(f32[4]{0:T(128)} %constant.4) | copy-start | bytes 52

commit v4 on v3

--- a/solution.py
+++ b/solution.py
@@ -824,33 +824,43 @@
             copy.start()
 
     ag.run(FIRST_ORDER if first_layer else LAST_ORDER, meanwhile, prepare, work)
-    copies = []
-    for j in range(1, levels):
-        l, l_dev = g.l_other(j)
-        near[j - 1] = total[pl.ds(pl.multiple_of(l * h, h), h), :].astype(BF16)
-        copy = pltpu.make_async_remote_copy(
-            near.at[j - 1], far.at[levels - 1 - j], near_send.at[j - 1], near_recv.at[levels - 1 - j], device_id=l_dev, device_id_type=MESH
-        )
-        copy.start()
-        copies.append(copy)
-    received = total[pl.ds(pl.multiple_of(g.l * h, h), h), :]
-    npre = dot(node[...].astype(BF16), nw1[:width, :]) + wide(nb1)
-    for copy in copies:
-        copy.wait()
-    for j in range(1, levels):
-        received = received + far[j - 1].astype(F32)
-    received = received.astype(BF16)
-    recv_out[...] = received
-    npre = npre + dot(received, nw1[width:, :])
-    npre_out[...] = npre
-    nnormed, nscale = norm_parts(dot((npre * lax.logistic(npre)).astype(BF16), nw2[...]) + wide(nb2))
-    nnormed_out[...] = nnormed
-    nscale_out[...] = jnp.broadcast_to(nscale, (h, 128))
-    change = nnormed * wide(ngain) + wide(nshift)
-    new = node[...] + change
-    node_out[...] = new
-    tally[0:8, :] = fold(new * new)
-    tally[24:32, :] = fold(change * change)
+    half = h // 2
+    copies = [[], []]
+    for part in range(2):
+        here = slice(part * half, (part + 1) * half)
+        for j in range(1, levels):
+            l, l_dev = g.l_other(j)
+            near[j - 1, here, :] = total[pl.ds(pl.multiple_of(l * h + part * half, half), half), :].astype(BF16)
+            copy = pltpu.make_async_remote_copy(
+                near.at[j - 1, pl.ds(part * half, half)],
+                far.at[levels - 1 - j, pl.ds(part * half, half)],
+                near_send.at[2 * (j - 1) + part],
+                near_recv.at[2 * (levels - 1 - j) + part],
+                device_id=l_dev,
+                device_id_type=MESH,
+            )
+            copy.start()
+            copies[part].append(copy)
+    npre_out[...] = dot(node[...].astype(BF16), nw1[:width, :]) + wide(nb1)
+    for part in range(2):
+        here = slice(part * half, (part + 1) * half)
+        received = total[pl.ds(pl.multiple_of(g.l * h + part * half, half), half), :]
+        for copy in copies[part]:
+            copy.wait()
+        for j in range(1, levels):
+            received = received + far[j - 1, here, :].astype(F32)
+        received = received.astype(BF16)
+        recv_out[here, :] = received
+        npre = npre_out[here, :] + dot(received, nw1[width:, :])
+        npre_out[here, :] = npre
+        nnormed, nscale = norm_parts(dot((npre * lax.logistic(npre)).astype(BF16), nw2[...]) + wide(nb2))
+        nnormed_out[here, :] = nnormed
+        nscale_out[here, :] = jnp.broadcast_to(nscale, (half, 128))
+        change = nnormed * wide(ngain) + wide(nshift)
+        new = node[here, :] + change
+        node_out[here, :] = new
+        tally[0:8, :] += fold(new * new)
+        tally[24:32, :] += fold(change * change)
     for n in range(2):
         for copy in leave(n, pl.ds(0, 2 * group)):
             copy.wait()
@@ -920,8 +930,8 @@
             pltpu.SemaphoreType.DMA((rows // 2,)),
             pltpu.SemaphoreType.DMA((Courier.sends(levels, rows, 2),)),
             pltpu.SemaphoreType.DMA((Courier.receives(levels, rows, 2),)),
-            pltpu.SemaphoreType.DMA((others,)),
-            pltpu.SemaphoreType.DMA((others,)),
+            pltpu.SemaphoreType.DMA((2 * others,)),
+            pltpu.SemaphoreType.DMA((2 * others,)),
         ]
         + scratch,
         compiler_params=pltpu.CompilerParams(collective_id=1 + layer, has_side_effects=True, vmem_limit_bytes=VMEM_BYTES),

time: 358 us -> 358 us (level)
  no operation moved by 1% of the time
where the time goes in v4:
time: 358 us; the launch traced here: 351 us
  Pallas kernels  348 us (97%)
    pallas_call x2, Pallas kernels, backward_layer(): pl.pallas_call(functools.partial(backward_kernel, layer, levels, rows, la...  123 us
    pallas_call x2, Pallas kernels, forward_layer(): pl.pallas_call(functools.partial(forward_kernel, layer, levels, rows, fir...  122 us
    pallas_call x1, Pallas kernels, sum_pieces(): pl.pallas_call(functools.partial(sum_kernel, levels, rows, h, len(terms))...  84 us
    pallas_call x1, Pallas kernels, finish_all(): pl.pallas_call(functools.partial(finish_kernel, parts, smalls), out_shape...  18.7 us

profile of v4, /device:TPU:0, one launch (start us, length us, event | category | flops | bytes accessed | tf_op | source)
XLA Modules:
  0.0 350.7 jit_solution(5025307181465255542)
XLA Ops:
  1.3 64.9 %forward_0.1 = (bf16[2560,512]{1,0:T(8,128)(2,1)}, bf16[2560,512]{1,0:T(8,128)(2,1)}, bf16[2560,512]{1,0:T(8,128)(2,1)}, bf16[2560,512]{1,0:T(8,128)(2,1)}, bf16...) custom-call(f32[512,512]{1,0:T(8,128)} %refs_0_.1, ...), custom_call_target="tpu_custom_call" | custom-call | tf_op jit(solution)/shard_map/forward_0/pallas_call | solution.py:909
  66.2 56.9 %forward_1.1 = (bf16[2560,512]{1,0:T(8,128)(2,1)}, bf16[2560,512]{1,0:T(8,128)(2,1)}, bf16[2560,512]{1,0:T(8,128)(2,1)}, bf16[2560,512]{1,0:T(8,128)(2,1)}, bf16...) custom-call(f32[256,512]{1,0:T(8,128)} %get-tuple-element.78.refs_0_, ...), custom_call_target="tpu_custom_call" | custom-call | tf_op jit(solution)/shard_map/forward_1/pallas_call | solution.py:909
  123.1 60.3 %backward_1.1 = (f32[256,512]{1,0:T(8,128)}, bf16[2560,512]{1,0:T(8,128)(2,1)}, bf16[2560,512]{1,0:T(8,128)(2,1)}, bf16[3584,512]{1,0:T(8,128)(2,1)}, f32[64,512]{1,0:T(8,128)}, /*index=5*/bf16[512,512]{1,0:T(8,128)(2,1)}) custom-call(f32[512,512]{1,0:T(8,128)} %d_node.1, bf16[512,512]{1,0:T(8,128)(2,1)} %get-tuple-element.84.block, ...), custom_call_target="tpu_custom_call" | custom-call | tf_op jit(solution)/shard_map/backward_1/pallas_call | solution.py:1108
  183.5 63.0 %backward_0.1 = (f32[256,512]{1,0:T(8,128)}, bf16[16,128]{1,0:T(8,128)(2,1)}, bf16[2560,512]{1,0:T(8,128)(2,1)}, bf16[3584,512]{1,0:T(8,128)(2,1)}, f32[64,512]{1,0:T(8,128)}, /*index=5*/bf16[16,128]{1,0:T(8,128)(2,1)}) custom-call(f32[256,512]{1,0:T(8,128)} %get-tuple-element.95.d_node, bf16[512,512]{1,0:T(8,128)(2,1)} %get-tuple-element.96.block, ...), custom_call_target="tpu_custom_call" | custom-call | tf_op jit(solution)/shard_map/backward_0/pallas_call | solution.py:1108
  246.5 84.0 %sum_5.1 = (bf16[7680,512]{1,0:T(8,128)(2,1)}, bf16[512,512]{1,0:T(8,128)(2,1)}, bf16[2560,512]{1,0:T(8,128)(2,1)}, bf16[2560,512]{1,0:T(8,128)(2,1)}) custom-call(f32[256,512]{1,0:T(8,128)} %get-tuple-element.108.refs_0_, s32[20,128]{1,0:T(8,128)} %get-tuple-element.79.refs_14_.refs_1_, f32[64,512]{1,0:T(8,128)} %get-tuple-element.109.refs_2_, ...), custom_call_target="tpu_custom_call" | custom-call | tf_op jit(solution)/shard_map/sum_5/pallas_call | solution.py:1243
  330.4 0.0 copy-start
  330.5 18.7 %finish_all.1 = (f32[2560,512]{1,0:T(8,128)}, f32[2560,512]{1,0:T(8,128)}, f32[2,1536,512]{2,1,0:T(8,128)}, f32[2,512,512]{2,1,0:T(8,128)}, f32[2,1024,512]{2,1,...) custom-call(bf16[2560,512]{1,0:T(8,128)(2,1)} %get-tuple-element.117, ...), custom_call_target="tpu_custom_call" | custom-call | tf_op jit(solution)/shard_map/finish_all/pallas_call | solution.py:1343
  349.2 0.6 slice_reduce_fusion
  349.8 0.1 reshape_squeeze.3
  349.9 0.0 copy-done
  349.9 0.6 multiply_sqrt_fusion
Async XLA Ops:
  330.4 19.5 %copy-start = (f32[4]{0:T(128)S(1)}, f32[4]{0:T(128)}, u32[]{:S(2)}) copy-start(f32[4]{0:T(128)} %constant.4) | copy-start | bytes 52
